TPU v7x, 256 devices: a whole 4x4x8 slice. The times are simulated.
256 devices in a mesh: rows: 8 (over x, core), clus: 32 (over y, z).
Axes of the slice: x: 4, y: 4, z: 8, core: 2. Of those that a mesh axis runs over, the one named last changes fastest.
Arguments:
- embed: bfloat16 [32768, 768], P(('rows', 'clus')), may hold values from -10 to 10
- weights: bfloat16 [32, 2736, 768], P('clus'), may hold values from -0.21875 to 0.21875
- shortlist: int32 [32768, 4], P(('rows', 'clus')), may hold values from 0 to 31, all different within a row; in each aligned block of 128 rows (0 to 127, 128 to 255, ...) at most 32 rows name the same one
- positives: int32 [32768, 8], P(('rows', 'clus')), may hold values from 0 to 10943
Outputs:
- row_grad: bfloat16 [32768, 768], P(('rows', 'clus'))
- row_loss: float32 [32768], P(('rows', 'clus'))
- weight_grad: bfloat16 [32, 2736, 768], P('clus', 'rows')
Inputs may be any that keep to these rules, and one draw needn't show every extreme that they name: `shortlist`: each row names 4 different clusters. Among the rows of one device no cluster is named by more than 32 rows, a bound that some block reaches. `positives`: entry j * 2736 + l names label l of the row's j-th shortlisted cluster; a row may repeat an entry.
All inputs are finite; a program needn't handle non-finite values.
Results may differ from a plain program's by a relative error of at most 0.0034.
Values may be sent and summed in bfloat16 or wider, within the bound.
No kernel may reach another device: no remote copies, remote signals or barrier semaphores. Data moves between devices by JAX's collectives and lax.ppermute only.
A program may use at most 128 MiB of HBM per device.

v0:
```python
import jax
import jax.numpy as jnp
from jax import lax
from jax.sharding import PartitionSpec as P


def bucket_positions(short_block, clusters, capacity):
    flat_ids = short_block.reshape(-1)
    onehot = (flat_ids[:, None] == jnp.arange(clusters, dtype=jnp.int32)[None, :]).astype(jnp.int32)
    running = jnp.cumsum(onehot, axis=0)
    ranked = jnp.sum(onehot * running, axis=1) - 1
    return flat_ids * capacity + ranked


def pair_offsets(positive_block, shortlist_k, labels):
    slot_iota = jnp.arange(shortlist_k, dtype=jnp.int32)
    inside = positive_block[:, None, :] // labels == slot_iota[None, :, None]
    offsets = jnp.where(inside, positive_block[:, None, :] % labels, -1)
    offsets = offsets.reshape(-1, positive_block.shape[1])
    return jnp.concatenate([offsets, jnp.full((1, positive_block.shape[1]), -1, jnp.int32)])


def score_cluster(rows_in, offsets_in, table):
    label_iota = jnp.arange(table.shape[0], dtype=jnp.int32)
    scores = jnp.dot(rows_in, table.T, preferred_element_type=jnp.float32)
    hits = jnp.zeros(scores.shape, dtype=bool)
    for column in range(offsets_in.shape[1]):
        hits = jnp.logical_or(hits, offsets_in[:, column : column + 1] == label_iota[None, :])
    target = hits.astype(jnp.float32)
    losses = jnp.sum(jax.nn.softplus(scores) - target * scores, axis=1)
    error = (jax.nn.sigmoid(scores) - target).astype(jnp.bfloat16)
    grads = jnp.dot(error, table, preferred_element_type=jnp.float32)
    return (error, grads, losses)


def answer(got_rows, got_offsets, weights, capacity):
    sources, _, width = got_rows.shape
    rows_in = got_rows.reshape(-1, width)
    offsets_in = got_offsets.reshape(-1, got_offsets.shape[2])
    error, grads, losses = score_cluster(rows_in, offsets_in, weights[0])
    grad_parts = grads.reshape(sources, capacity, width)
    loss_parts = losses.reshape(sources, capacity)
    errors = [error]
    inputs = [rows_in]
    return (grad_parts, loss_parts, errors, inputs)


def local(embed, weights, shortlist, positives):
    row_dev, width = embed.shape
    shortlist_k = shortlist.shape[1]
    clus_dev, labels, _ = weights.shape
    groups = lax.axis_size("clus")
    clusters = clus_dev * groups
    capacity = 2 * row_dev * shortlist_k // clusters
    pair_count = row_dev * shortlist_k
    all_rows, all_short, all_positive = (
        lax.all_gather(embed, "clus", axis=0, tiled=True),
        lax.all_gather(shortlist, "clus", axis=0, tiled=True),
        lax.all_gather(positives, "clus", axis=0, tiled=True),
    )
    owner = lax.axis_index("clus")
    source_positions = jax.vmap(lambda block: bucket_positions(block, clusters, capacity))(
        all_short.reshape(groups, row_dev, shortlist_k)
    )
    local_slots = source_positions - owner * clus_dev * capacity
    owned = jnp.logical_and(local_slots >= 0, local_slots < clus_dev * capacity)
    target_slots = jnp.where(owned, local_slots, clus_dev * capacity)
    source_ids = jnp.broadcast_to(
        jnp.arange(groups, dtype=jnp.int32)[:, None], (groups, pair_count)
    )
    pair_ids = jnp.broadcast_to(
        jnp.arange(pair_count, dtype=jnp.int32)[None, :], (groups, pair_count)
    )
    tables = (
        jnp.full((groups, clus_dev * capacity), pair_count, jnp.int32)
        .at[source_ids, target_slots]
        .set(pair_ids, mode="drop")
    )
    source_rows = jnp.concatenate(
        [all_rows.reshape(groups, row_dev, width), jnp.zeros((groups, 1, width), embed.dtype)],
        axis=1,
    )
    picks = jnp.where(tables < pair_count, tables // shortlist_k, row_dev)
    got_rows = jnp.take_along_axis(source_rows, picks[:, :, None], axis=1)
    source_offsets = jax.vmap(lambda block: pair_offsets(block, shortlist_k, labels))(
        all_positive.reshape(groups, row_dev, -1)
    )
    got_offsets = jnp.take_along_axis(source_offsets, tables[:, :, None], axis=1)
    partial_grads, partial_loss, errors, inputs = answer(got_rows, got_offsets, weights, capacity)
    summed_grads = jax.vmap(
        lambda grads, picked: jnp.zeros((row_dev + 1, width), jnp.float32).at[picked].add(grads)
    )(partial_grads, picks)
    summed_loss = jax.vmap(
        lambda losses, picked: jnp.zeros((row_dev + 1,), jnp.float32).at[picked].add(losses)
    )(partial_loss, picks)
    summed_grads = summed_grads[:, :row_dev].reshape(groups * row_dev, width)
    summed_loss = summed_loss[:, :row_dev].reshape(groups * row_dev)
    row_grad, row_total = (
        lax.psum_scatter(summed_grads, "clus", scatter_dimension=0, tiled=True),
        lax.psum_scatter(summed_loss, "clus", scatter_dimension=0, tiled=True),
    )
    pieces = []
    for error, rows_in in zip(errors, inputs):
        pieces.append(
            lax.dot_general(
                error, rows_in, (((0,), (0,)), ((), ())), preferred_element_type=jnp.float32
            )
        )
    share = lax.psum_scatter(jnp.stack(pieces, axis=1), "rows", scatter_dimension=0, tiled=True)
    weight_grad = jnp.transpose(share, (1, 0, 2)).astype(jnp.bfloat16)
    return (row_grad.astype(jnp.bfloat16), row_total / (shortlist_k * labels), weight_grad)


def solution(mesh):
    placed = (
        P(("rows", "clus"), None),
        P("clus", None, None),
        P(("rows", "clus"), None),
        P(("rows", "clus"), None),
    )
    return jax.shard_map(
        local,
        mesh=mesh,
        in_specs=placed,
        out_specs=(P(("rows", "clus"), None), P(("rows", "clus")), P("clus", "rows", None)),
        check_vma=False,
    )
```

profile of v0, /device:TPU:2, one launch (start us, length us, event | category | flops | bytes accessed | tf_op | source)
XLA Modules:
  0.0 1242.7 jit_solution(6811315471863302032)
XLA Ops:
  8.0 52.1 %all_gather.9 = s32[4096,4]{0,1:T(4,128)S(1)} all-gather(s32[128,4]{0,1:T(4,128)} %param.6), channel_id=1, replica_groups=mesh['rows'=8,'clus'=32] {'clus'}, dimensions={0}, use_global_device_ids=true | all-gather | bytes 67584 | tf_op jit(solution)/shard_map/all_gather | solution.py:58
  64.3 42.4 %all_gather.11 = s32[4096,8]{0,1:T(8,128)S(1)} all-gather(s32[128,8]{0,1:T(8,128)S(1)} %copy-done.1), channel_id=1, replica_groups=mesh['rows'=8,'clus'=32] {'clus'}, dimensions={0}, use_global_device_ids=true | all-gather | bytes 135168 | tf_op jit(solution)/shard_map/all_gather | solution.py:59
  106.8 2.8 copy.50
  113.6 64.4 %reduce-window.6 = s32[32,32,4,128]{3,1,2,0:T(8,128)S(1)} reduce-window(s32[32,32,4,128]{3,1,2,0:T(8,128)} %fusion.17, s32[]{:T(128)} %constant.80.clone.1), window={size=1x1x1x128 pad=0_0x0_0x0_0x127_0}, to_apply=%region_0.0 | reduce-window | flops 66584576 | bytes 4194308 | tf_op jit(solution)/shard_map/reduce-window
  179.9 2.4 copy.46
  183.5 60.5 %scatter_custom_fusion = s32[1024]{0:T(1024)S(1)} fusion(s32[16384]{0:T(1024)S(1)} %bitcast.103, s32[16384]{0:T(1024)S(1)} %bitcast.102, s32[]{:T(128)} %constant.51.clone.1), kind=kCustom, calls=%fused_computation.98 | custom fusion | bytes 4100
  244.6 2.8 copy.51
  247.4 2.8 bitcast_select_fusion
  250.2 4.3 concatenate.11
  254.5 14.9 %gather_fusion.1 = s32[1024,8]{1,0:T(8,128)S(1)} fusion(s32[32,513,8]{2,0,1:T(8,128)} %concatenate.11, s32[1024]{0:T(1024)S(1)} %reshape.238), kind=kCustom, calls=%fused_computation.1 | custom fusion | bytes 73728 | tf_op jit(solution)/shard_map/jit(take_along_axis)/gather | solution.py:88
  271.7 6.3 copy.49
  278.0 3.2 concatenate.10
  281.2 25.7 %gather_fusion = bf16[1024,768]{1,0:T(8,128)(2,1)S(1)} fusion(bf16[32,129,768]{2,0,1:T(8,128)(2,1)} %concatenate.10, s32[1024]{0:T(1024)S(1)} %reshape.232), kind=kCustom, calls=%fused_computation | custom fusion | bytes 3153920 | tf_op jit(solution)/shard_map/jit(take_along_axis)/gather | solution.py:84
  307.1 21.1 %fusion.1 = (f32[1024]{0:T(1024)S(1)}, bf16[1024,2736]{0,1:T(8,128)(2,1)}) fusion(s32[1024]{0:T(1024)S(1)} %get-tuple-element.4, s32[1024]{0:T(1024)S(1)} %get-tuple-element.5, s32[1024]{0:T(1024)S(1)} %get-tuple-element.6, s32[1024]{0:T(1024)S(1)} %get-tuple-element.7, s32[1024]{0:T(1024)S(1)} %get-tuple-element.8, s32[1024]{0:T(1024)S(1)} %get-tuple-element.9, ...), kind=kOutput, calls=%fused_computation.7 | convolution fusion | flops 4387404800 | bytes 11415552 | tf_op jit(solution)/shard_map/dot_general | solution.py:25
  328.2 8.3 copy.52
  336.5 10.1 fusion.11
  346.7 13.8 %scatter_custom_fusion.1 = f32[4128,768]{1,0:T(8,128)} fusion(s32[1024]{0:T(1024)S(1)} %reshape.250, f32[1024,768]{1,0:T(8,128)} %bitcast.104, f32[]{:T(128)} %constant.50.clone.1), kind=kCustom, calls=%fused_computation.26 | custom fusion | flops 786432 | bytes 12681728
  360.5 10.7 slice.62
  371.2 16.4 %copy.53 = f32[32,128,768]{2,1,0:T(8,128)} copy(f32[32,128,768]{2,0,1:T(8,128)} %slice.62) | data formatting | bytes 25165824 | tf_op jit(solution)/shard_map/slice | solution.py:96
  390.8 7.8 scatter_custom_fusion.2
  398.8 6.9 convolution_bitcast_fusion
  405.7 18.4 %copy.54 = f32[2736,1,768]{2,1,0:T(1,128)} copy(f32[2736,1,768]{2,0,1:T(8,128)S(1)} %convolution_bitcast_fusion) | data formatting | bytes 16809984 | tf_op jit(solution)/shard_map/stack | solution.py:109
  424.1 662.6 %all-reduce.5 = bf16[2736,1,768]{2,1,0:T(2,128)(2,1)} all-reduce(f32[2736,1,768]{2,1,0:T(1,128)} %copy.54), channel_id=4, replica_groups=mesh['rows'=8,'clus'=32] {'rows'}, use_global_device_ids=true, to_apply=%region_9.10.clone | all-reduce | flops 2101248 | bytes 12607488
  1089.9 143.4 %all-reduce.2 = f32[4096]{0:T(1024)S(1)} all-reduce(f32[4096]{0:T(1024)S(1)} %slice_bitcast_fusion), channel_id=3, replica_groups=mesh['rows'=8,'clus'=32] {'clus'}, use_global_device_ids=true, to_apply=%region_8.9.clone | all-reduce | flops 4096 | bytes 32768
  (70 shorter events, 22.7 us)
Async XLA Ops:
  7.2 57.1 %copy-start.1 = (s32[128,8]{0,1:T(8,128)S(1)}, s32[128,8]{0,1:T(8,128)}, u32[]{:S(2)}) copy-start(s32[128,8]{0,1:T(8,128)} %param.7) | copy-start | bytes 12292
  7.2 264.5 %all-gather.2.cloned.1.call-start = ((), (), s32[]{:S(2)}) async-start(), calls=%async_computation.1 | async-start | bytes 6488064 | tf_op jit(solution)/shard_map/all_gather | solution.py:57
  7.9 1226.0 %reduce-scatter.2.cloned.1.call-start = ((), (), s32[]{:S(2)}) async-start(), calls=%async_computation.2 | async-start | bytes 12976128 | tf_op jit(solution)/shard_map/reduce_scatter | solution.py:99
  178.0 5.4 copy-start.5
  178.0 66.2 %copy-start.4 = (s32[2]{0:T(128)S(1)}, s32[2]{0:T(128)}, u32[]{:S(2)}) copy-start(s32[2]{0:T(128)} %constant.112) | copy-start | bytes 28
  178.0 66.3 %copy-start.2 = (s32[2]{0:T(128)S(1)}, s32[2]{0:T(128)}, u32[]{:S(2)}) copy-start(s32[2]{0:T(128)} %constant.115) | copy-start | bytes 28
  178.0 66.3 %copy-start.3 = (s32[2]{0:T(128)S(1)}, s32[2]{0:T(128)}, u32[]{:S(2)}) copy-start(s32[2]{0:T(128)} %constant.109) | copy-start | bytes 28
  183.2 64.2 %copy-start = (s32[32,128,8]{2,0,1:T(8,128)S(1)}, s32[32,128,8]{2,0,1:T(8,128)}, u32[]{:S(2)}) copy-start(s32[32,128,8]{2,0,1:T(8,128)} %copy.50) | copy-start | bytes 393220
  387.6 0.7 copy-start.7
  387.6 1.3 copy-start.6
Sparse Core Ops, SparseCore 0:
  10.6 92.2 all-gather.1
  387.8 237.8 reduce-scatter.1
where the time goes:
time: 1260 us; the launch traced here: 1240 us
  blocking collectives  901 us (72%)
  local copies, waits for them, and re-layouts  193 us (15%)
  other arithmetic  94.5 us (8%)
  matrix products  38.1 us (3%)
  between operations  15.8 us (1%)
    unnamed x2, blocking collectives  806 us
    unnamed x25, local copies, waits for them, and re-layouts  64.7 us
    another operation x2, other arithmetic  64.5 us
    all_gather x1, blocking collectives, local(): lax.all_gather(shortlist, 'clus', axis=0, tiled=True)  52.1 us
    all_gather x1, blocking collectives, local(): lax.all_gather(positives, 'clus', axis=0, tiled=True)  42.4 us
    slice x2, local copies, waits for them, and re-layouts, local(): summed_grads = summed_grads[:, :row_dev].reshape(groups * row_dev, width)  27.1 us
    gather x1, local copies, waits for them, and re-layouts, local(): got_rows = jnp.take_along_axis(source_rows, picks[:, :, None], axis=1)  25.7 us
  transfers between devices with their start and end apart: 2, of which 0 were waited for; matrix products, arithmetic and copies ran while one was open for 17% of the time, Pallas kernels for 0%

commit v1 on v0

v1 whole, which is shorter than its diff:
```python
import functools
import jax
import jax.numpy as jnp
from jax import lax
from jax.experimental import pallas as pl
from jax.experimental.pallas import tpu as pltpu
from jax.sharding import PartitionSpec as P

BF = jnp.bfloat16
F32 = jnp.float32
LANES = 128
CHUNK = 256
HALF = 16
VMEM_LIMIT = 56 * 1024 * 1024

NT = (((1,), (1,)), ((), ()))
TN = (((0,), (0,)), ((), ()))
NN = (((1,), (0,)), ((), ()))


def dot(a, b, dims=NN):
    return lax.dot_general(a, b, dims, preferred_element_type=F32)


def iota(shape, dim):
    return lax.broadcasted_iota(jnp.int32, shape, dim)


def padded(block):
    return -(-block // 32) * 32


def pack_kernel(labels, shards, embed_ref, short_ref, pos_ref, send_ref, pick_ref):
    rows, width = embed_ref.shape
    slots_k = short_ref.shape[0]
    clusters = send_ref.shape[0]
    cap = 2 * HALF
    block = labels // shards
    extra = padded(block) - block
    short = short_ref[...]
    pos = pos_ref[...]
    count = pos.shape[0]
    cluster_id = iota((clusters, rows), 0)
    member = jnp.zeros((clusters, rows), F32)
    for j in range(slots_k):
        member += (short[j : j + 1, :] == cluster_id).astype(F32)
    before = (iota((rows, rows), 0) < iota((rows, rows), 1)).astype(BF)
    rank = dot(member.astype(BF), before)
    code = jnp.where(member > 0.5, rank, -1.0)
    slot = iota((clusters, cap, rows), 1).astype(F32)
    pick = (code[:, None, :] == slot).astype(F32)
    pick = pick.reshape(clusters * cap, rows).astype(BF)
    pick_ref[...] = pick
    values, names = [], []
    for j in range(slots_k):
        local = pos - j * labels
        inside = jnp.logical_and(local >= 0, local < labels)
        shard = jnp.zeros_like(local)
        for b in range(1, shards):
            shard += (local >= b * block).astype(jnp.int32)
        column = jnp.where(inside, local + extra * shard, 0)
        bit = lax.shift_left(jnp.ones_like(column), lax.shift_right_logical(column, 7))
        values.append(jnp.where(inside, bit, 0).astype(F32))
        values.append(jnp.bitwise_and(column, LANES - 1).astype(F32))
        names.append(jnp.broadcast_to(short[j : j + 1, :], (2 * count, rows)).astype(F32))
    used = 2 * count * slots_k
    rest = jnp.zeros((LANES - used, rows), F32)
    values = jnp.concatenate(values + [rest], axis=0).astype(BF)
    names = jnp.concatenate(names + [rest], axis=0).astype(BF)
    got_values = dot(pick, values, NT)
    got_names = dot(pick, names, NT)
    own = lax.shift_right_logical(iota(got_values.shape, 0), 5).astype(F32)
    kept = jnp.where(got_names == own, got_values, 0.0).astype(BF)
    kept = kept.reshape(clusters, cap, LANES)
    source = iota((LANES, LANES), 0)
    target = iota((LANES, LANES), 1)
    folded = jnp.bitwise_and(source, 2 * count - 1)
    valid = source < used
    fold_a = jnp.logical_and(valid, folded == target).astype(BF)
    fold_b = jnp.logical_and(valid, folded + 2 * count == target).astype(BF)
    meta = dot(kept[:, :HALF].reshape(clusters * HALF, LANES), fold_a)
    meta += dot(kept[:, HALF:].reshape(clusters * HALF, LANES), fold_b)
    got = dot(pick, embed_ref[...]).astype(BF).reshape(clusters, cap, width)
    send_ref[:, :, :width] = got[:, :HALF]
    send_ref[:, :, width : 2 * width] = got[:, HALF:]
    send_ref[:, :, 2 * width :] = meta.astype(BF).reshape(clusters, HALF, LANES)


def log1p(p):
    small = p * (1.0 - p * (0.5 - p * (1.0 / 3.0 - p * 0.25)))
    return jnp.where(p < 0.01, small, jnp.log(1.0 + p))


def compute_kernel(
    count, core_ref, recv_ref, weight_ref, real_ref, back_ref, keep_ref, give_ref,
    rows_ref, bits_ref, s_a, s_b, e_a, e_b, grad_ref, wgrad_ref, relu_ref, prod_ref,
):
    sources = recv_ref.shape[0]
    width = rows_ref.shape[1]
    total = rows_ref.shape[0]
    chunks = weight_ref.shape[0] // CHUNK
    rows3 = jnp.concatenate(
        [recv_ref[:, :, :width], recv_ref[:, :, width : 2 * width]], axis=1
    )
    rows_ref[...] = rows3.reshape(total, width)
    step = 8
    for start in range(0, sources, step):
        meta = recv_ref[start : start + step, :, 2 * width :].astype(F32).astype(jnp.int32)
        meta = meta.reshape(step * HALF, LANES)
        lane = iota((step * HALF, LANES), 1)
        halves = []
        for base in (0, 2 * count):
            bits = jnp.zeros((step * HALF, LANES), jnp.int32)
            for p in range(count):
                value = meta[:, base + p : base + p + 1]
                place = meta[:, base + count + p : base + count + p + 1]
                bits = jnp.bitwise_or(bits, jnp.where(place == lane, value, 0))
            halves.append(bits.reshape(step, HALF, LANES))
        both = jnp.concatenate(halves, axis=1)
        bits_ref[start * 2 * HALF : (start + step) * 2 * HALF] = both.reshape(-1, LANES)
    grad_ref[...] = jnp.zeros_like(grad_ref)
    relu_ref[...] = jnp.zeros_like(relu_ref)
    prod_ref[...] = jnp.zeros_like(prod_ref)

    def weight(i):
        return weight_ref[pl.ds(pl.multiple_of(i * CHUNK, CHUNK), CHUNK), :]

    def score(i, s_ref):
        s_ref[...] = dot(rows_ref[...], weight(i), NT)

    def pointwise(i, s_ref, e_ref):
        tall = 64
        for start in range(0, total, tall):
            here = slice(start, start + tall)
            bits = bits_ref[here]
            relu = relu_ref[here]
            prod = prod_ref[here]
            for part in range(CHUNK // LANES):
                lanes = slice(part * LANES, (part + 1) * LANES)
                real = real_ref[i * (CHUNK // LANES) + part]
                s = s_ref[here, lanes]
                hit = lax.shift_left(bits, 31 - (i * (CHUNK // LANES) + part)) < 0
                v = jnp.where(hit, -s, s)
                e = jnp.exp(-jnp.abs(s))
                d = 1.0 + e
                r = pl.reciprocal(d, approx=True)
                r = r * (2.0 - d * r)
                sig = jnp.where(v >= 0.0, r, e * r)
                e_ref[here, lanes] = jnp.where(hit, -sig, sig).astype(BF)
                relu = relu + jnp.maximum(v, 0.0)
                prod = prod + (e * real) * (1.0 + prod)
            relu_ref[here] = relu
            prod_ref[here] = prod

    def gradients(i, e_ref):
        e = e_ref[...]
        grad_ref[...] += dot(e, weight(i))
        wgrad_ref[pl.ds(pl.multiple_of(i * CHUNK, CHUNK), CHUNK), :] = dot(e, rows_ref[...], TN)

    score(0, s_a)
    score(1, s_b)
    pointwise(0, s_a, e_a)

    def pair(k, carry):
        i = 2 * k + 1
        score(i + 1, s_a)
        pointwise(i, s_b, e_b)
        gradients(i - 1, e_a)
        score(i + 2, s_b)
        pointwise(i + 1, s_a, e_a)
        gradients(i, e_b)
        return carry

    lax.fori_loop(0, (chunks - 3) // 2, pair, 0)
    last = chunks - 1
    score(last, s_a)
    pointwise(last - 1, s_b, e_b)
    gradients(last - 2, e_a)
    pointwise(last, s_a, e_a)
    gradients(last - 1, e_b)
    gradients(last, e_a)

    grads = grad_ref[...].astype(BF).reshape(sources, 2 * HALF, width)
    back_ref[:, :, :width] = grads[:, :HALF]
    back_ref[:, :, width : 2 * width] = grads[:, HALF:]
    loss = jnp.sum(relu_ref[...] + log1p(prod_ref[...]), axis=1, keepdims=True)
    first = loss.astype(BF).astype(F32)
    second = (loss - first).astype(BF).astype(F32)
    third = loss - first - second
    lane = iota((total, LANES), 1)
    part = jnp.bitwise_and(lane, 3)
    terms = jnp.where(part == 0, first, jnp.where(part == 1, second, jnp.where(part == 2, third, 0.0)))
    terms = terms.reshape(sources, 2 * HALF, LANES)
    side = iota((sources, HALF, LANES), 2)
    mixed = jnp.where(
        side < 4, terms[:, :HALF], jnp.where(side < 8, terms[:, HALF:], 0.0)
    )
    back_ref[:, :, 2 * width :] = mixed.astype(BF)

    me = core_ref[0]
    shards, block, _ = keep_ref.shape
    for x in range(shards):
        mine = pl.multiple_of((2 * x + me) * block, 32)
        other = pl.multiple_of((2 * x + 1 - me) * block, 32)
        keep_ref[x] = wgrad_ref[pl.ds(mine, block), :]
        give_ref[x] = wgrad_ref[pl.ds(other, block), :].astype(BF)


def combine_kernel(scale, got_ref, pick_ref, grad_ref, loss_ref):
    clusters = got_ref.shape[0]
    width = grad_ref.shape[1]
    rows = grad_ref.shape[0]
    pick = pick_ref[...].reshape(clusters, 2 * HALF, rows)
    pick_a = pick[:, :HALF].reshape(clusters * HALF, rows)
    pick_b = pick[:, HALF:].reshape(clusters * HALF, rows)

    def lanes(start, size):
        return got_ref[:, :, start : start + size].reshape(clusters * HALF, size)

    grads = dot(pick_a, lanes(0, width), TN) + dot(pick_b, lanes(width, width), TN)
    grad_ref[...] = grads.astype(BF)
    terms = lanes(2 * width, LANES)
    first = dot(terms, pick_a, TN)
    second = dot(terms, pick_b, TN)
    loss = jnp.sum(first[:4], axis=0, keepdims=True) + jnp.sum(second[4:8], axis=0, keepdims=True)
    loss_ref[...] = loss * scale


def whole(shape, dtype):
    return jax.ShapeDtypeStruct(shape, dtype)


VM = pl.BlockSpec(memory_space=pltpu.VMEM)
SM = pl.BlockSpec(memory_space=pltpu.SMEM)
PARAMS = pltpu.CompilerParams(vmem_limit_bytes=VMEM_LIMIT)


def local(embed, weights, shortlist, positives):
    rows, width = embed.shape
    slots_k = shortlist.shape[1]
    count = positives.shape[1]
    _, labels, _ = weights.shape
    clusters = lax.axis_size("clus")
    shards = lax.axis_size("rows")
    wide = 2 * width + LANES
    total = clusters * 2 * HALF
    block = labels // shards
    tall = padded(block)
    half = shards // 2

    send, pick = pl.pallas_call(
        functools.partial(pack_kernel, labels, shards),
        out_shape=(whole((clusters, HALF, wide), BF), whole((total, rows), BF)),
        in_specs=[VM] * 3,
        out_specs=(VM, VM),
        compiler_params=PARAMS,
    )(embed, shortlist.T, positives.T)
    recv = lax.all_to_all(send, "clus", 0, 0, tiled=True)

    table = jnp.pad(weights.reshape(shards, block, width), ((0, 0), (0, tall - block), (0, 0)))
    table = table.reshape(shards * tall, width)
    column = jnp.arange(shards * tall, dtype=jnp.int32)
    real = (column % tall < block).astype(F32).reshape(-1, 1, LANES)
    place = lax.axis_index("rows")
    core = place % 2
    back, keep, give = pl.pallas_call(
        functools.partial(compute_kernel, count),
        out_shape=(
            whole((clusters, HALF, wide), BF),
            whole((half, tall, width), F32),
            whole((half, tall, width), BF),
        ),
        in_specs=[SM, VM, VM, VM],
        out_specs=(VM, VM, VM),
        scratch_shapes=[
            pltpu.VMEM((total, width), BF),
            pltpu.VMEM((total, LANES), jnp.int32),
            pltpu.VMEM((total, CHUNK), F32),
            pltpu.VMEM((total, CHUNK), F32),
            pltpu.VMEM((total, CHUNK), BF),
            pltpu.VMEM((total, CHUNK), BF),
            pltpu.VMEM((total, width), F32),
            pltpu.VMEM((shards * tall, width), F32),
            pltpu.VMEM((total, LANES), F32),
            pltpu.VMEM((total, LANES), F32),
        ],
        compiler_params=PARAMS,
    )(core.reshape(1), recv, table, real)

    taken = lax.ppermute(give, "rows", [(i, i ^ 1) for i in range(shards)])
    pair = keep + taken.astype(F32)
    x = place // 2

    def piece(k):
        return lax.dynamic_index_in_dim(pair, (x + k) % half, 0, keepdims=False)

    share = piece(0)
    arrived = []
    for k in range(1, half):
        perm = [(i, (i + 2 * k) % shards) for i in range(shards)]
        arrived.append(lax.ppermute(piece(k).astype(BF), "rows", perm))

    got = lax.all_to_all(back, "clus", 0, 0, tiled=True)
    row_grad, row_loss = pl.pallas_call(
        functools.partial(combine_kernel, 1.0 / (slots_k * labels)),
        out_shape=(whole((rows, width), BF), whole((1, rows), F32)),
        in_specs=[VM] * 2,
        out_specs=(VM, VM),
        compiler_params=PARAMS,
    )(got, pick)

    for part in arrived:
        share = share + part.astype(F32)
    weight_grad = share[:block].astype(BF)[None]
    return row_grad, row_loss.reshape(rows), weight_grad


def solution(mesh):
    placed = (
        P(("rows", "clus"), None),
        P("clus", None, None),
        P(("rows", "clus"), None),
        P(("rows", "clus"), None),
    )
    return jax.shard_map(
        local,
        mesh=mesh,
        in_specs=placed,
        out_specs=(P(("rows", "clus"), None), P(("rows", "clus")), P("clus", "rows", None)),
        check_vma=False,
    )
```

time: 1260 us -> 139 us (0.11); the launches traced: 1240 us -> 139 us
  blocking collectives: 901 us -> 0 us
  local copies, waits for them, and re-layouts: 193 us -> 14.5 us
  other arithmetic: 94.5 us -> 6.41 us
  waiting for transfers between devices: 0.72 us -> 61.8 us
  matrix products: 38.1 us -> 0 us
  Pallas kernels: 0 us -> 34.1 us
  starting transfers between devices: 0.08 us -> 21.4 us
  between operations: 15.8 us -> 0.77 us
    unnamed x2 -> x0, blocking collectives: 806 us -> none
    all_gather x2 -> x0, blocking collectives: 94.5 us -> none  [the longest x1 52.1 us: local(): lax.all_gather(shortlist, 'clus', axis=0, tiled=True)]
    another operation x2 -> x0, other arithmetic: 64.5 us -> none
    unnamed x25 -> x6, local copies, waits for them, and re-layouts: 64.7 us -> 4.39 us
    gather x3 -> x0, local copies, waits for them, and re-layouts: 40.6 us -> none  [the longest x1 25.7 us: local(): got_rows = jnp.take_along_axis(source_rows, picks[:, :, None], axis=1)]
    all_to_all x0 -> x2, waiting for transfers between devices: none -> 39.3 us  [the longest x1 32.7 us: local(): recv = lax.all_to_all(send, 'clus', 0, 0, tiled=True)]
    dot_general x3 -> x0, matrix products: 38.1 us -> none  [the longest x1 21.1 us: score_cluster(): scores = jnp.dot(rows_in, table.T, preferred_element_type=jnp.float32)]
    pallas_call x0 -> x3, Pallas kernels: none -> 34.1 us  [the longest x1 28.3 us: local(): pl.pallas_call(functools.partial(compute_kernel, count), out_shape=(whole...]
  transfers between devices with their start and end apart: 2 -> 6, of which waited for: 0 -> 5; matrix products, arithmetic and copies ran while one was open for 17% -> 12% of each run, Pallas kernels for 0% -> 0%
where the time goes in v1:
time: 139 us
  waiting for transfers between devices  61.8 us (44%)
  Pallas kernels  34.1 us (25%)
  starting transfers between devices  21.4 us (15%)
  local copies, waits for them, and re-layouts  14.5 us (10%)
  other arithmetic  6.41 us (5%)
    all_to_all x1, waiting for transfers between devices, local(): recv = lax.all_to_all(send, 'clus', 0, 0, tiled=True)  32.7 us
    pallas_call x1, Pallas kernels, local(): pl.pallas_call(functools.partial(compute_kernel, count), out_shape=(whole...  28.3 us
    ppermute x3, waiting for transfers between devices, local(): arrived.append(lax.ppermute(piece(k).astype(BF), 'rows', perm))  22.5 us
    all_to_all x1, starting transfers between devices, local(): recv = lax.all_to_all(send, 'clus', 0, 0, tiled=True)  11.5 us
    all_to_all x1, waiting for transfers between devices, local(): got = lax.all_to_all(back, 'clus', 0, 0, tiled=True)  6.56 us
    all_to_all x1, starting transfers between devices, local(): got = lax.all_to_all(back, 'clus', 0, 0, tiled=True)  5.74 us
    pad x1, local copies, waits for them, and re-layouts, local(): jnp.pad(weights.reshape(shards, block, width), ((0, 0), (0, tall - block)...  4.47 us
    unnamed x6, local copies, waits for them, and re-layouts  4.39 us
  transfers between devices with their start and end apart: 6, of which 5 were waited for; matrix products, arithmetic and copies ran while one was open for 12% of the time, Pallas kernels for 0%

profile of v1, /device:TPU:2, one launch (start us, length us, event | category | flops | bytes accessed | tf_op | source)
XLA Modules:
  0.0 139.0 jit_solution(1633152482246286187)
XLA Ops:
  0.6 3.2 %shard_map.67 = (bf16[32,16,1664]{2,1,0:T(8,128)(2,1)}, bf16[1024,128]{1,0:T(8,128)(2,1)}) custom-call(bf16[128,768]{1,0:T(8,128)(2,1)} %embed_ref.1, s32[4,128]{1,0:T(4,128)} %bitcast.17, s32[8,128]{1,0:T(8,128)} %bitcast.16), custom_call_target="tpu_custom_call" | custom-call | tf_op jit(solution)/shard_map/pallas_call | solution.py:251
  3.8 11.5 %all-to-all-start = ((bf16[32,16,1664]{2,1,0:T(8,128)(2,1)}), bf16[32,16,1664]{2,1,0:T(8,128)(2,1)S(1)}, u32[]{:S(2)}, u32[]{:S(2)}) async-start(bf16[32,16,1664]{2,1,0:T(8,128)(2,1)} %get-tuple-element.10), calls=%async_computation | async-start | bytes 3407872 | tf_op jit(solution)/shard_map/all_to_all | solution.py:258
  15.3 4.2 %reshape.60 = bf16[8,342,768]{2,1,0:T(8,128)(2,1)} reshape(bf16[1,2736,768]{2,1,0:T(8,128)(2,1)} %param.5) | data formatting | bytes 8404992 | tf_op jit(solution)/shard_map/reshape | solution.py:260
  19.5 4.5 %pad.4 = bf16[8,352,768]{2,1,0:T(8,128)(2,1)} pad(bf16[8,342,768]{2,1,0:T(8,128)(2,1)} %reshape.60, bf16[]{:T(256)} %constant.77.clone.1), padding=0_0x0_10x0_0 | pad | bytes 8527874 | tf_op jit(solution)/shard_map/jit(_pad)/pad | solution.py:260
  23.9 0.6 compare_convert_fusion.real_ref
  24.6 32.7 %all-to-all-done.recv_ref = bf16[32,16,1664]{2,1,0:T(8,128)(2,1)S(1)} async-done(((bf16[32,16,1664]{2,1,0:T(8,128)(2,1)}), bf16[32,16,1664]{2,1,0:T(8,128)(2,1)S(1)}, u32[]{:S(2)}, u32[]{:S(2)}) %all-to-all-start) | async-done | bytes 1703968 | tf_op jit(solution)/shard_map/all_to_all | solution.py:258
  57.3 1.2 copy-done.2
  58.5 28.3 %shard_map.68 = (bf16[32,16,1664]{2,1,0:T(8,128)(2,1)}, f32[4,352,768]{2,1,0:T(8,128)}, bf16[4,352,768]{2,1,0:T(8,128)(2,1)}) custom-call(s32[1]{0:T(128)} %bitcast.core_ref, bf16[32,16,1664]{2,1,0:T(8,128)(2,1)} %copy-done.2, bf16[2816,768]{1,0:T(8,128)(2,1)} %bitcast.15, f32[22,1,128]{2,1,0:T(1,128)} %compare_convert_fusion.real_ref), custom_call_target="tpu_custom_call" | custom-call | tf_op jit(solution)/shard_map/pallas_call | solution.py:266
  86.8 5.7 %all-to-all-start.1 = ((bf16[32,16,1664]{2,1,0:T(8,128)(2,1)}), bf16[32,16,1664]{2,1,0:T(8,128)(2,1)S(1)}, u32[]{:S(2)}, u32[]{:S(2)}) async-start(bf16[32,16,1664]{2,1,0:T(8,128)(2,1)} %get-tuple-element.11), calls=%async_computation.1 | async-start | bytes 3407872 | tf_op jit(solution)/shard_map/all_to_all | solution.py:303
  92.7 0.0 collective-permute-done
  92.7 3.3 %convert_add_fusion = f32[4,352,768]{2,1,0:T(8,128)S(1)} fusion(f32[4,352,768]{2,1,0:T(8,128)} %get-tuple-element.15, bf16[4,352,768]{2,1,0:T(8,128)(2,1)} %collective-permute-done), kind=kLoop, calls=%fused_computation | loop fusion | flops 2162688 | bytes 10813440 | tf_op jit(solution)/shard_map/add | solution.py:291
  96.0 2.0 %copy-done = f32[4,352,768]{2,1,0:T(8,128)} copy-done((f32[4,352,768]{2,1,0:T(8,128)}, f32[4,352,768]{2,1,0:T(8,128)S(1)}, u32[]{:S(2)}) %copy-start) | copy-done | bytes 4325400
  98.0 0.2 fusion.3
  98.2 1.6 %collective-permute-start.1 = (bf16[352,768]{1,0:T(8,128)(2,1)S(1)}, bf16[352,768]{1,0:T(8,128)(2,1)}, u32[]{:S(2)}, u32[]{:S(2)}) collective-permute-start(bf16[352,768]{1,0:T(8,128)(2,1)S(1)} %get-tuple-element.17), channel_id=1, source_target_pairs={{0,64},{32,96},{64,128},{96,160},{128,192},{160,224},{192,0},{224,... | collective-permute-start | bytes 1622024 | tf_op jit(solution)/shard_map/ppermute | solution.py:301
  99.7 0.5 collective-permute-start.3
  100.3 2.1 %collective-permute-start.2 = (bf16[352,768]{1,0:T(8,128)(2,1)S(1)}, bf16[352,768]{1,0:T(8,128)(2,1)}, u32[]{:S(2)}, u32[]{:S(2)}) collective-permute-start(bf16[352,768]{1,0:T(8,128)(2,1)S(1)} %get-tuple-element.19), channel_id=1, source_target_pairs={{0,128},{32,160},{64,192},{96,224},{128,0},{160,32},{192,64},{224,... | collective-permute-start | bytes 1622024 | tf_op jit(solution)/shard_map/ppermute | solution.py:301
  102.4 1.3 dynamic-slice_bitcast_fusion
  103.7 9.8 %collective-permute-done.1 = bf16[352,768]{1,0:T(8,128)(2,1)} collective-permute-done((bf16[352,768]{1,0:T(8,128)(2,1)S(1)}, bf16[352,768]{1,0:T(8,128)(2,1)}, u32[]{:S(2)}, u32[]{:S(2)}) %collective-permute-start.1) | collective-permute-done | bytes 540704 | tf_op jit(solution)/shard_map/ppermute | solution.py:301
  113.5 0.9 collective-permute-done.3
  114.4 11.8 %collective-permute-done.2 = bf16[352,768]{1,0:T(8,128)(2,1)} collective-permute-done((bf16[352,768]{1,0:T(8,128)(2,1)S(1)}, bf16[352,768]{1,0:T(8,128)(2,1)}, u32[]{:S(2)}, u32[]{:S(2)}) %collective-permute-start.2) | collective-permute-done | bytes 540704 | tf_op jit(solution)/shard_map/ppermute | solution.py:301
  126.2 2.4 %fusion.6 = bf16[1,342,768]{2,1,0:T(8,128)(2,1)} fusion(f32[352,768]{1,0:T(8,128)S(1)} %dynamic-slice_bitcast_fusion, bf16[352,768]{1,0:T(8,128)(2,1)} %collective-permute-done.3, bf16[352,768]{1,0:T(8,128)(2,1)} %collective-permute-done.2, bf16[352,768]{1,0:T(8,128)(2,1)} %collective-permute-done.1), kind=kLoop, calls=%fused_computation.12 | loop fusion | flops 1838592 | bytes 3151872 | tf_op jit(solution)/shard_map/broadcast_in_dim | solution.py:314
  128.6 6.6 %all-to-all-done.1.got_ref = bf16[32,16,1664]{2,1,0:T(8,128)(2,1)S(1)} async-done(((bf16[32,16,1664]{2,1,0:T(8,128)(2,1)}), bf16[32,16,1664]{2,1,0:T(8,128)(2,1)S(1)}, u32[]{:S(2)}, u32[]{:S(2)}) %all-to-all-start.1) | async-done | bytes 1703968 | tf_op jit(solution)/shard_map/all_to_all | solution.py:303
  135.2 1.2 copy-done.1
  136.4 2.6 %shard_map.69 = (bf16[128,768]{1,0:T(8,128)(2,1)}, f32[1,128]{1,0:T(1,128)}) custom-call(bf16[32,16,1664]{2,1,0:T(8,128)(2,1)} %copy-done.1, bf16[1024,128]{1,0:T(8,128)(2,1)} %get-tuple-element.12.pick_ref), custom_call_target="tpu_custom_call" | custom-call | tf_op jit(solution)/shard_map/pallas_call | solution.py:304
  (4 shorter events, 0.0 us)
Async XLA Ops:
  3.8 53.5 %all-to-all-start = ((bf16[32,16,1664]{2,1,0:T(8,128)(2,1)}), bf16[32,16,1664]{2,1,0:T(8,128)(2,1)S(1)}, u32[]{:S(2)}, u32[]{:S(2)}) async-start(bf16[32,16,1664]{2,1,0:T(8,128)(2,1)} %get-tuple-element.10), calls=%async_computation | async-start | bytes 3407872 | tf_op jit(solution)/shard_map/all_to_all | solution.py:258
  57.3 1.2 copy-start.2
  86.8 5.8 %collective-permute-start = (bf16[4,352,768]{2,1,0:T(8,128)(2,1)}, bf16[4,352,768]{2,1,0:T(8,128)(2,1)}, u32[]{:S(2)}, u32[]{:S(2)}) collective-permute-start(bf16[4,352,768]{2,1,0:T(8,128)(2,1)} %get-tuple-element.16), channel_id=1, source_target_pairs={{0,32},{32,0},{64,96},{96,64},{128,160},{160,128},{192,224},{224,1... | collective-permute-start | bytes 6488072 | tf_op jit(solution)/shard_map/ppermute | solution.py:290
  86.8 48.3 %all-to-all-start.1 = ((bf16[32,16,1664]{2,1,0:T(8,128)(2,1)}), bf16[32,16,1664]{2,1,0:T(8,128)(2,1)S(1)}, u32[]{:S(2)}, u32[]{:S(2)}) async-start(bf16[32,16,1664]{2,1,0:T(8,128)(2,1)} %get-tuple-element.11), calls=%async_computation.1 | async-start | bytes 3407872 | tf_op jit(solution)/shard_map/all_to_all | solution.py:303
  96.0 2.0 %copy-start = (f32[4,352,768]{2,1,0:T(8,128)}, f32[4,352,768]{2,1,0:T(8,128)S(1)}, u32[]{:S(2)}) copy-start(f32[4,352,768]{2,1,0:T(8,128)S(1)} %convert_add_fusion) | copy-start | bytes 12976132
  98.2 15.3 %collective-permute-start.1 = (bf16[352,768]{1,0:T(8,128)(2,1)S(1)}, bf16[352,768]{1,0:T(8,128)(2,1)}, u32[]{:S(2)}, u32[]{:S(2)}) collective-permute-start(bf16[352,768]{1,0:T(8,128)(2,1)S(1)} %get-tuple-element.17), channel_id=1, source_target_pairs={{0,64},{32,96},{64,128},{96,160},{128,192},{160,224},{192,0},{224,... | collective-permute-start | bytes 1622024 | tf_op jit(solution)/shard_map/ppermute | solution.py:301
  99.7 14.6 %collective-permute-start.3 = (bf16[352,768]{1,0:T(8,128)(2,1)S(1)}, bf16[352,768]{1,0:T(8,128)(2,1)}, u32[]{:S(2)}, u32[]{:S(2)}) collective-permute-start(bf16[352,768]{1,0:T(8,128)(2,1)S(1)} %get-tuple-element.18), channel_id=1, source_target_pairs={{0,192},{32,224},{64,0},{96,32},{128,64},{160,96},{192,128},{224,1... | collective-permute-start | bytes 1622024 | tf_op jit(solution)/shard_map/ppermute | solution.py:301
  100.3 25.9 %collective-permute-start.2 = (bf16[352,768]{1,0:T(8,128)(2,1)S(1)}, bf16[352,768]{1,0:T(8,128)(2,1)}, u32[]{:S(2)}, u32[]{:S(2)}) collective-permute-start(bf16[352,768]{1,0:T(8,128)(2,1)S(1)} %get-tuple-element.19), channel_id=1, source_target_pairs={{0,128},{32,160},{64,192},{96,224},{128,0},{160,32},{192,64},{224,... | collective-permute-start | bytes 1622024 | tf_op jit(solution)/shard_map/ppermute | solution.py:301
  135.2 1.2 copy-start.1

commit v2 on v1

v2 whole, which is shorter than its diff:
```python
import functools
import jax
import jax.numpy as jnp
import numpy as np
from jax import lax
from jax.experimental import pallas as pl
from jax.experimental.pallas import tpu as pltpu
from jax.sharding import PartitionSpec as P

BF = jnp.bfloat16
F32 = jnp.float32
LANES = 128
CHUNK = 256
HALF = 16
VMEM_LIMIT = 40 * 1024 * 1024
TALL = 32
BLOCK = 512
LOG2E = 1.4426950408889634

NT = (((1,), (1,)), ((), ()))
TN = (((0,), (0,)), ((), ()))
NN = (((1,), (0,)), ((), ()))


def dot(a, b, dims=NN):
    return lax.dot_general(a, b, dims, preferred_element_type=F32)


def iota(shape, dim):
    return lax.broadcasted_iota(jnp.int32, shape, dim)


def padded(block):
    return -(-block // 32) * 32


def pack_kernel(labels, shards, shift_ref, embed_ref, short_ref, pos_ref, send_ref, pick_ref):
    rows, width = embed_ref.shape
    slots_k = short_ref.shape[0]
    clusters = send_ref.shape[0]
    cap = 2 * HALF
    block = labels // shards
    short = short_ref[...]
    pos = pos_ref[...]
    count = pos.shape[0]
    cluster_id = iota((clusters, rows), 0)
    member = jnp.zeros((clusters, rows), F32)
    for j in range(slots_k):
        member += (short[j : j + 1, :] == cluster_id).astype(F32)
    before = (iota((rows, rows), 0) < iota((rows, rows), 1)).astype(BF)
    rank = dot(member.astype(BF), before)
    code = jnp.where(member > 0.5, rank, -1.0)
    slot = iota((clusters, cap, rows), 1).astype(F32)
    pick = (code[:, None, :] == slot).astype(F32)
    pick = pick.reshape(clusters * cap, rows).astype(BF)
    pick_ref[...] = pick
    values, names = [], []
    for j in range(slots_k):
        local = pos - j * labels
        inside = jnp.logical_and(local >= 0, local < labels)
        column = local + shift_ref[0]
        for b in range(1, shards):
            column += jnp.where(local >= b * block, shift_ref[b] - shift_ref[b - 1], 0)
        column = jnp.where(inside, column, 0)
        bit = lax.shift_left(jnp.ones_like(column), lax.shift_right_logical(column, 7))
        values.append(jnp.where(inside, bit, 0).astype(F32))
        values.append(jnp.bitwise_and(column, LANES - 1).astype(F32))
        names.append(jnp.broadcast_to(short[j : j + 1, :], (2 * count, rows)).astype(F32))
    used = 2 * count * slots_k
    rest = jnp.zeros((LANES - used, rows), F32)
    values = jnp.concatenate(values + [rest], axis=0).astype(BF)
    names = jnp.concatenate(names + [rest], axis=0).astype(BF)
    got_values = dot(pick, values, NT)
    got_names = dot(pick, names, NT)
    own = lax.shift_right_logical(iota(got_values.shape, 0), 5).astype(F32)
    kept = jnp.where(got_names == own, got_values, 0.0).astype(BF)
    kept = kept.reshape(clusters, cap, LANES)
    source = iota((LANES, LANES), 0)
    target = iota((LANES, LANES), 1)
    folded = jnp.bitwise_and(source, 2 * count - 1)
    valid = source < used
    fold_a = jnp.logical_and(valid, folded == target).astype(BF)
    fold_b = jnp.logical_and(valid, folded + 2 * count == target).astype(BF)
    meta = dot(kept[:, :HALF].reshape(clusters * HALF, LANES), fold_a)
    meta += dot(kept[:, HALF:].reshape(clusters * HALF, LANES), fold_b)
    got = dot(pick, embed_ref[...]).astype(BF).reshape(clusters, cap, width)
    send_ref[:, :, :width] = got[:, :HALF]
    send_ref[:, :, width : 2 * width] = got[:, HALF:]
    send_ref[:, :, 2 * width :] = meta.astype(BF).reshape(clusters, HALF, LANES)


def assemble(recv_ref, rows_ref):
    total, width = rows_ref.shape
    left, right = recv_ref[:, :, :width], recv_ref[:, :, width : 2 * width]
    rows_ref[...] = jnp.concatenate([left, right], axis=1).reshape(total, width)


def target_bits(count, recv_ref, bits_ref, width):
    sources = recv_ref.shape[0]
    step = 8
    for start in range(0, sources, step):
        meta = recv_ref[start : start + step, :, 2 * width :].astype(F32).astype(jnp.int32)
        meta = meta.reshape(step * HALF, LANES)
        lane = iota((step * HALF, LANES), 1)
        halves = []
        for base in (0, 2 * count):
            bits = jnp.zeros((step * HALF, LANES), jnp.int32)
            for p in range(count):
                value = meta[:, base + p : base + p + 1]
                place = meta[:, base + count + p : base + count + p + 1]
                bits = jnp.bitwise_or(bits, jnp.where(place == lane, value, 0))
            halves.append(bits.reshape(step, HALF, LANES))
        both = jnp.concatenate(halves, axis=1)
        bits_ref[start * 2 * HALF : (start + step) * 2 * HALF] = both.reshape(-1, LANES)


def score_kernel(
    count, recv_ref, weight_ref, pads_ref, back_ref, error_out,
    rows_ref, bits_ref, s_ref, error_ref, relu_ref, prod_ref, sum_ref, sem,
):
    sources = recv_ref.shape[0]
    total, width = rows_ref.shape
    chunks = weight_ref.shape[0] // CHUNK
    assemble(recv_ref, rows_ref)
    target_bits(count, recv_ref, bits_ref, width)
    copies = []

    def score(i, at):
        chunk = weight_ref[i * CHUNK : (i + 1) * CHUNK]
        s_ref[i % 2, at] = dot(rows_ref[at], chunk, NT)

    def pointwise(i, at):
        for start in range(at.start, at.stop, TALL):
            here = slice(start, start + TALL)
            bits = bits_ref[here]
            if i == 0:
                relu = jnp.zeros((TALL, LANES), F32)
                prod = jnp.ones((TALL, LANES), F32)
                summed = relu
            else:
                relu, prod, summed = relu_ref[here], prod_ref[here], sum_ref[here]
            for part in range(CHUNK // LANES):
                column = i * CHUNK + part * LANES
                s = s_ref[i % 2, here, part * LANES : (part + 1) * LANES]
                hit = lax.shift_left(bits, 31 - column // LANES) < 0
                size = jnp.abs(s)
                e = jnp.exp2(size * -LOG2E)
                d = 1.0 + e
                r = pl.reciprocal(d, approx=True)
                up = jnp.logical_xor(s >= 0.0, hit)
                chance = jnp.where(up, r, e * r)
                error = jnp.where(hit, -chance, chance)
                error_ref[here, column : column + LANES] = error.astype(BF)
                relu = relu + jnp.where(up, size, 0.0)
                prod = prod * d
                summed = summed + e
            relu_ref[here] = relu
            prod_ref[here] = prod
            sum_ref[here] = summed

    blocks = [slice(k, k + BLOCK) for k in range(0, total, BLOCK)]
    for i in range(-1, chunks):
        for at in blocks:
            if i + 1 < chunks:
                score(i + 1, at)
            if i >= 0:
                pointwise(i, at)
        if i >= 0:
            columns = slice(i * CHUNK, (i + 1) * CHUNK)
            copy = pltpu.make_async_copy(
                error_ref.at[:, columns], error_out.at[:, columns], sem.at[i]
            )
            copy.start()
            copies.append(copy)
    for at in blocks:
        first, last = at.start // (2 * HALF), at.stop // (2 * HALF)
        grads = dot(error_ref[at], weight_ref[...]).astype(BF)
        grads = grads.reshape(last - first, 2 * HALF, width)
        back_ref[first:last, :, :width] = grads[:, :HALF]
        back_ref[first:last, :, width : 2 * width] = grads[:, HALF:]

    summed = sum_ref[...] - pads_ref[0:1]
    tail = jnp.where(summed < 4e-4, summed, jnp.log(prod_ref[...] * pads_ref[1:2]))
    loss = jnp.sum(relu_ref[...] + tail, axis=1, keepdims=True)
    first = loss.astype(BF).astype(F32)
    second = (loss - first).astype(BF).astype(F32)
    third = loss - first - second
    part = jnp.bitwise_and(iota((total, LANES), 1), 3)
    terms = jnp.where(part == 2, third, 0.0)
    terms = jnp.where(part == 1, second, terms)
    terms = jnp.where(part == 0, first, terms)
    terms = terms.reshape(sources, 2 * HALF, LANES)
    side = iota((sources, HALF, LANES), 2)
    mixed = jnp.where(side < 8, terms[:, HALF:], 0.0)
    mixed = jnp.where(side < 4, terms[:, :HALF], mixed)
    back_ref[:, :, 2 * width :] = mixed.astype(BF)
    for copy in copies:
        copy.wait()


def weight_kernel(error_ref, recv_ref, out_ref, rows_ref):
    assemble(recv_ref, rows_ref)
    labels = out_ref.shape[0]
    for start in range(0, labels, 2 * CHUNK):
        here = slice(start, min(start + 2 * CHUNK, labels))
        out_ref[here] = dot(error_ref[:, here], rows_ref[...], TN).astype(out_ref.dtype)


def combine_kernel(scale, got_ref, pick_ref, grad_ref, loss_ref):
    clusters = got_ref.shape[0]
    width = grad_ref.shape[1]
    rows = grad_ref.shape[0]
    pick = pick_ref[...].reshape(clusters, 2 * HALF, rows)
    pick_a = pick[:, :HALF].reshape(clusters * HALF, rows)
    pick_b = pick[:, HALF:].reshape(clusters * HALF, rows)

    def lanes(start, size):
        return got_ref[:, :, start : start + size].reshape(clusters * HALF, size)

    grads = dot(pick_a, lanes(0, width), TN) + dot(pick_b, lanes(width, width), TN)
    grad_ref[...] = grads.astype(BF)
    terms = lanes(2 * width, LANES)
    first = dot(terms, pick_a, TN)
    second = dot(terms, pick_b, TN)
    loss = jnp.sum(first[:4], axis=0, keepdims=True) + jnp.sum(second[4:8], axis=0, keepdims=True)
    loss_ref[...] = loss * scale


def whole(shape, dtype):
    return jax.ShapeDtypeStruct(shape, dtype)


VM = pl.BlockSpec(memory_space=pltpu.VMEM)
SM = pl.BlockSpec(memory_space=pltpu.SMEM)
PARAMS = pltpu.CompilerParams(vmem_limit_bytes=VMEM_LIMIT)


def local(embed, weights, shortlist, positives):
    rows, width = embed.shape
    slots_k = shortlist.shape[1]
    count = positives.shape[1]
    _, labels, _ = weights.shape
    clusters = lax.axis_size("clus")
    shards = lax.axis_size("rows")
    wide = 2 * width + LANES
    total = clusters * 2 * HALF
    block = labels // shards
    tall = padded(block)
    half = shards // 2

    place = lax.axis_index("rows")
    core, x = place % 2, place // 2
    order = [((x + k) % half) * 2 + side for side in (1 - core, core) for k in range(half)]
    shard = jnp.arange(shards, dtype=jnp.int32)
    step = (shard // 2 - x + half) % half
    slot = jnp.where(shard % 2 == core, half + step, step)
    shift = (tall * slot - block * shard).astype(jnp.int32)

    send, pick = pl.pallas_call(
        functools.partial(pack_kernel, labels, shards),
        out_shape=(whole((clusters, HALF, wide), BF), whole((total, rows), BF)),
        in_specs=[SM] + [VM] * 3,
        out_specs=(VM, VM),
        compiler_params=PARAMS,
    )(shift, embed, shortlist.T, positives.T)
    recv = lax.all_to_all(send, "clus", 0, 0, tiled=True)

    table = jnp.pad(weights.reshape(shards, block, width), ((0, 0), (0, tall - block), (0, 0)))
    table = jnp.stack([lax.dynamic_index_in_dim(table, k, 0, keepdims=False) for k in order])
    table = table.reshape(shards * tall, width)
    column = np.arange(shards * tall)
    pads = np.bincount(column[column % tall >= block] % LANES, minlength=LANES)
    pads = np.stack([pads, 0.5**pads]).astype(np.float32)
    back, error = pl.pallas_call(
        functools.partial(score_kernel, count),
        out_shape=(whole((clusters, HALF, wide), BF), whole((total, shards * tall), BF)),
        in_specs=[VM, VM, VM],
        out_specs=(VM, pl.BlockSpec(memory_space=pl.ANY)),
        scratch_shapes=[
            pltpu.VMEM((total, width), BF),
            pltpu.VMEM((total, LANES), jnp.int32),
            pltpu.VMEM((2, total, CHUNK), F32),
            pltpu.VMEM((total, shards * tall), BF),
            pltpu.VMEM((total, LANES), F32),
            pltpu.VMEM((total, LANES), F32),
            pltpu.VMEM((total, LANES), F32),
            pltpu.SemaphoreType.DMA((shards * tall // CHUNK,)),
        ],
        compiler_params=PARAMS,
    )(recv, table, jnp.asarray(pads))
    got = lax.all_to_all(back, "clus", 0, 0, tiled=True)

    def weight_part(index, dtype):
        size = half * tall
        work = total * size * width
        return pl.pallas_call(
            weight_kernel,
            grid=(1,),
            out_shape=whole((size, width), dtype),
            in_specs=[
                pl.BlockSpec((total, size), lambda i: (0, index)),
                pl.BlockSpec((clusters, HALF, wide), lambda i: (0, 0, 0)),
            ],
            out_specs=pl.BlockSpec((size, width), lambda i: (0, 0)),
            scratch_shapes=[pltpu.VMEM((total, width), BF)],
            compiler_params=PARAMS,
            cost_estimate=pl.CostEstimate(
                flops=2 * work, bytes_accessed=8 * 1024 * 1024, transcendentals=0
            ),
        )(error, recv)

    give = weight_part(0, BF)
    taken = lax.ppermute(give, "rows", [(i, i ^ 1) for i in range(shards)])
    keep = weight_part(1, F32)

    def piece(k):
        here = slice(k * tall, (k + 1) * tall)
        return keep[here] + taken[here].astype(F32)

    arrived = []
    for k in (2, 1, 3):
        perm = [(i, (i + 2 * k) % shards) for i in range(shards)]
        arrived.append(lax.ppermute(piece(k).astype(BF), "rows", perm))
    share = piece(0)

    row_grad, row_loss = pl.pallas_call(
        functools.partial(combine_kernel, 1.0 / (slots_k * labels)),
        out_shape=(whole((rows, width), BF), whole((1, rows), F32)),
        in_specs=[VM] * 2,
        out_specs=(VM, VM),
        compiler_params=PARAMS,
    )(got, pick)

    for part in arrived:
        share = share + part.astype(F32)
    weight_grad = share[:block].astype(BF)[None]
    return row_grad, row_loss.reshape(rows), weight_grad


def solution(mesh):
    placed = (
        P(("rows", "clus"), None),
        P("clus", None, None),
        P(("rows", "clus"), None),
        P(("rows", "clus"), None),
    )
    return jax.shard_map(
        local,
        mesh=mesh,
        in_specs=placed,
        out_specs=(P(("rows", "clus"), None), P(("rows", "clus")), P("clus", "rows", None)),
        check_vma=False,
    )
```

time: 139 us -> 133 us (0.957)
  Pallas kernels: 34.1 us -> 26.9 us
  other arithmetic: 6.41 us -> 2.94 us
  local copies, waits for them, and re-layouts: 14.5 us -> 17.7 us
    unnamed x6 -> x31, local copies, waits for them, and re-layouts: 4.39 us -> 12.5 us
    pallas_call x1 -> x3, Pallas kernels: 28.3 us -> 23 us  [the longest x1 16.7 us: local(): pl.pallas_call(functools.partial(score_kernel, count), out_shape=(whole((...]
    pad x1 -> x0, local copies, waits for them, and re-layouts: 4.47 us -> none  [local(): jnp.pad(weights.reshape(shards, block, width), ((0, 0), (0, tall - block)...]
    add x1 -> x0, other arithmetic: 3.34 us -> none  [local(): pair = keep + taken.astype(F32)]
    pallas_call x1, Pallas kernels: 2.61 us -> 1.15 us  [local(): pl.pallas_call(functools.partial(combine_kernel, 1.0 / (slots_k * labels)...]
  transfers between devices with their start and end apart: 6 -> 6, of which waited for: 5 -> 5; matrix products, arithmetic and copies ran while one was open for 12% -> 7% of each run, Pallas kernels for 0% -> 2%
where the time goes in v2:
time: 133 us; the launch traced here: 132 us
  waiting for transfers between devices  62.2 us (47%)
  Pallas kernels  26.9 us (20%)
  starting transfers between devices  21.4 us (16%)
  local copies, waits for them, and re-layouts  17.7 us (13%)
  other arithmetic  2.94 us (2%)
    all_to_all x1, waiting for transfers between devices, local(): recv = lax.all_to_all(send, 'clus', 0, 0, tiled=True)  33.1 us
    ppermute x3, waiting for transfers between devices, local(): arrived.append(lax.ppermute(piece(k).astype(BF), 'rows', perm))  22.4 us
    pallas_call x1, Pallas kernels, local(): pl.pallas_call(functools.partial(score_kernel, count), out_shape=(whole((...  16.7 us
    unnamed x31, local copies, waits for them, and re-layouts  12.5 us
    all_to_all x1, starting transfers between devices, local(): recv = lax.all_to_all(send, 'clus', 0, 0, tiled=True)  11.5 us
    all_to_all x1, waiting for transfers between devices, local(): got = lax.all_to_all(back, 'clus', 0, 0, tiled=True)  6.8 us
    pallas_call x2, Pallas kernels, weight_part(): pl.pallas_call(weight_kernel, grid=(1,), out_shape=whole((size, width), d...  6.34 us
    all_to_all x1, starting transfers between devices, local(): got = lax.all_to_all(back, 'clus', 0, 0, tiled=True)  5.72 us
  transfers between devices with their start and end apart: 6, of which 5 were waited for; matrix products, arithmetic and copies ran while one was open for 7% of the time, Pallas kernels for 2%

profile of v2, /device:TPU:2, one launch (start us, length us, event | category | flops | bytes accessed | tf_op | source)
XLA Modules:
  0.0 132.1 jit_solution(12251807113083478939)
XLA Ops:
  0.7 0.9 copy-done.7
  1.6 0.7 copy-done.8
  3.0 2.7 %shard_map.76 = (bf16[32,16,1664]{2,1,0:T(8,128)(2,1)}, bf16[1024,128]{1,0:T(8,128)(2,1)S(1)}) custom-call(s32[8]{0:T(128)S(1)} %fusion.20.shift_ref, bf16[128,768]{1,0:T(8,128)(2,1)S(1)} %copy-done.7, s32[4,128]{1,0:T(4,128)S(1)} %bitcast.8, s32[8,128]{1,0:T(8,128)S(1)} %bitcast.7), custom_call_target="tpu_custom_call" | custom-call | tf_op jit(solution)/shard_map/pallas_call | solution.py:259
  6.4 11.5 %all-to-all-start = ((bf16[32,16,1664]{2,1,0:T(8,128)(2,1)}), bf16[32,16,1664]{2,1,0:T(8,128)(2,1)S(1)}, u32[]{:S(2)}, u32[]{:S(2)}) async-start(bf16[32,16,1664]{2,1,0:T(8,128)(2,1)} %get-tuple-element.9), calls=%async_computation | async-start | bytes 3407872 | tf_op jit(solution)/shard_map/all_to_all | solution.py:266
  18.0 4.1 %reshape.15 = bf16[8,342,768]{2,1,0:T(8,128)(2,1)} reshape(bf16[1,2736,768]{2,1,0:T(8,128)(2,1)} %param.6) | data formatting | bytes 8404992 | tf_op jit(solution)/shard_map/reshape | solution.py:268
  22.1 1.2 fusion.7
  23.3 1.1 copy-done.11
  24.8 2.0 %copy-done.2 = bf16[8,352,768]{2,1,0:T(8,128)(2,1)} copy-done((bf16[8,352,768]{2,1,0:T(8,128)(2,1)}, bf16[8,352,768]{2,1,0:T(8,128)(2,1)S(1)}, u32[]{:S(2)}) %copy-start.2) | copy-done | bytes 4325400
  26.8 33.1 %all-to-all-done.recv_ref = bf16[32,16,1664]{2,1,0:T(8,128)(2,1)S(1)} async-done(((bf16[32,16,1664]{2,1,0:T(8,128)(2,1)}), bf16[32,16,1664]{2,1,0:T(8,128)(2,1)S(1)}, u32[]{:S(2)}, u32[]{:S(2)}) %all-to-all-start) | async-done | bytes 1703968 | tf_op jit(solution)/shard_map/all_to_all | solution.py:266
  59.9 2.2 %copy-done.3 = bf16[8,352,768]{2,1,0:T(8,128)(2,1)S(1)} copy-done((bf16[8,352,768]{2,1,0:T(8,128)(2,1)S(1)}, bf16[8,352,768]{2,1,0:T(8,128)(2,1)}, u32[]{:S(2)}) %copy-start.3) | copy-done | bytes 4325400
  62.1 16.7 %shard_map.77 = (bf16[32,16,1664]{2,1,0:T(8,128)(2,1)S(1)}, bf16[1024,2816]{1,0:T(8,128)(2,1)S(1)}) custom-call(bf16[32,16,1664]{2,1,0:T(8,128)(2,1)S(1)} %all-to-all-done.recv_ref, bf16[2816,768]{1,0:T(8,128)(2,1)S(1)} %bitcast.6, f32[2,128]{1,0:T(2,128)S(1)} %copy-done.10), custom_call_target="tpu_custom_call" | custom-call | tf_op jit(solution)/shard_map/pallas_call | solution.py:274
  78.8 3.9 %shard_map.80 = bf16[1408,768]{1,0:T(8,128)(2,1)} custom-call(bf16[1024,2816]{1,0:T(8,128)(2,1)S(1)} %get-tuple-element.14.error_ref, bf16[32,16,1664]{2,1,0:T(8,128)(2,1)S(1)} %all-to-all-done.recv_ref), custom_call_target="tpu_custom_call" | custom-call | flops 2214592512 | bytes 8388608 | tf_op jit(solution)/shard_map/pallas_call | solution.py:296
  82.7 5.7 %all-to-all-start.1 = ((bf16[32,16,1664]{2,1,0:T(8,128)(2,1)}), bf16[32,16,1664]{2,1,0:T(8,128)(2,1)S(1)}, u32[]{:S(2)}, u32[]{:S(2)}) async-start(bf16[32,16,1664]{2,1,0:T(8,128)(2,1)} %copy-done.4), calls=%async_computation.1 | async-start | bytes 3407872 | tf_op jit(solution)/shard_map/all_to_all | solution.py:291
  88.4 2.6 %copy-done.1 = bf16[1024,2816]{1,0:T(8,128)(2,1)S(1)} copy-done((bf16[1024,2816]{1,0:T(8,128)(2,1)S(1)}, bf16[1024,2816]{1,0:T(8,128)(2,1)}, u32[]{:S(2)}) %copy-start.1) | copy-done | bytes 5767192
  91.0 2.5 %shard_map.79 = f32[1408,768]{1,0:T(8,128)S(1)} custom-call(bf16[1024,2816]{1,0:T(8,128)(2,1)S(1)} %copy-done.1, bf16[32,16,1664]{2,1,0:T(8,128)(2,1)S(1)} %all-to-all-done.recv_ref), custom_call_target="tpu_custom_call" | custom-call | flops 2214592512 | bytes 8388608 | tf_op jit(solution)/shard_map/pallas_call | solution.py:296
  93.5 1.8 %fusion.2 = (bf16[352,768]{1,0:T(8,128)(2,1)S(1)}, bf16[352,768]{1,0:T(8,128)(2,1)S(1)}, bf16[352,768]{1,0:T(8,128)(2,1)S(1)}, f32[352,768]{1,0:T(8,128)S(1)}) fusion(f32[1408,768]{1,0:T(8,128)S(1)} %shard_map.79, bf16[1408,768]{1,0:T(8,128)(2,1)} %collective-permute-done), kind=kLoop, calls=%fused_computation.13 | loop fusion | flops 2433024 | bytes 8650752 | tf_op jit(solution)/shard_map/convert_element_type | solution.py:323
  95.3 2.2 %collective-permute-start.1 = (bf16[352,768]{1,0:T(8,128)(2,1)S(1)}, bf16[352,768]{1,0:T(8,128)(2,1)S(1)}, u32[]{:S(2)}, u32[]{:S(2)}) collective-permute-start(bf16[352,768]{1,0:T(8,128)(2,1)S(1)} %get-tuple-element.15), channel_id=1, source_target_pairs={{0,128},{32,160},{64,192},{96,224},{128,0},{160,32},{192,64},{224,... | collective-permute-start | bytes 1622024 | tf_op jit(solution)/shard_map/ppermute | solution.py:323
  97.5 1.5 %collective-permute-start.3 = (bf16[352,768]{1,0:T(8,128)(2,1)S(1)}, bf16[352,768]{1,0:T(8,128)(2,1)S(1)}, u32[]{:S(2)}, u32[]{:S(2)}) collective-permute-start(bf16[352,768]{1,0:T(8,128)(2,1)S(1)} %get-tuple-element.16), channel_id=1, source_target_pairs={{0,192},{32,224},{64,0},{96,32},{128,64},{160,96},{192,128},{224,1... | collective-permute-start | bytes 1622024 | tf_op jit(solution)/shard_map/ppermute | solution.py:323
  99.6 1.1 slice.38
  100.6 11.4 %collective-permute-done.1 = bf16[352,768]{1,0:T(8,128)(2,1)S(1)} collective-permute-done((bf16[352,768]{1,0:T(8,128)(2,1)S(1)}, bf16[352,768]{1,0:T(8,128)(2,1)S(1)}, u32[]{:S(2)}, u32[]{:S(2)}) %collective-permute-start.1) | collective-permute-done | bytes 540704 | tf_op jit(solution)/shard_map/ppermute | solution.py:323
  112.1 10.8 %collective-permute-done.3 = bf16[352,768]{1,0:T(8,128)(2,1)S(1)} collective-permute-done((bf16[352,768]{1,0:T(8,128)(2,1)S(1)}, bf16[352,768]{1,0:T(8,128)(2,1)S(1)}, u32[]{:S(2)}, u32[]{:S(2)}) %collective-permute-start.3) | collective-permute-done | bytes 540704 | tf_op jit(solution)/shard_map/ppermute | solution.py:323
  123.0 1.1 fusion.15
  124.1 6.8 %all-to-all-done.1.got_ref = bf16[32,16,1664]{2,1,0:T(8,128)(2,1)S(1)} async-done(((bf16[32,16,1664]{2,1,0:T(8,128)(2,1)}), bf16[32,16,1664]{2,1,0:T(8,128)(2,1)S(1)}, u32[]{:S(2)}, u32[]{:S(2)}) %all-to-all-start.1) | async-done | bytes 1703968 | tf_op jit(solution)/shard_map/all_to_all | solution.py:291
  131.0 1.2 shard_map.78
  (30 shorter events, 2.4 us)
Async XLA Ops:
  0.7 0.9 copy-start.7
  1.6 0.7 copy-start.8
  2.3 0.7 copy-start.9
  5.7 0.7 copy-start.5
  6.4 53.5 %all-to-all-start = ((bf16[32,16,1664]{2,1,0:T(8,128)(2,1)}), bf16[32,16,1664]{2,1,0:T(8,128)(2,1)S(1)}, u32[]{:S(2)}, u32[]{:S(2)}) async-start(bf16[32,16,1664]{2,1,0:T(8,128)(2,1)} %get-tuple-element.9), calls=%async_computation | async-start | bytes 3407872 | tf_op jit(solution)/shard_map/all_to_all | solution.py:266
  22.1 2.4 %copy-start.11 = (bf16[8,342,768]{2,1,0:T(8,128)(2,1)S(1)}, bf16[8,342,768]{2,1,0:T(8,128)(2,1)}, u32[]{:S(2)}) copy-start(bf16[8,342,768]{2,1,0:T(8,128)(2,1)} %reshape.15) | copy-start | bytes 12607492
  24.7 35.2 %copy-start.10 = (f32[2,128]{1,0:T(2,128)S(1)}, f32[2,128]{1,0:T(2,128)}, u32[]{:S(2)}) copy-start(f32[2,128]{1,0:T(2,128)} %constant.116.clone.pads_ref) | copy-start | bytes 3076
  24.8 2.0 %copy-start.2 = (bf16[8,352,768]{2,1,0:T(8,128)(2,1)}, bf16[8,352,768]{2,1,0:T(8,128)(2,1)S(1)}, u32[]{:S(2)}) copy-start(bf16[8,352,768]{2,1,0:T(8,128)(2,1)S(1)} %fusion.14) | copy-start | bytes 12976132
  59.9 2.2 %copy-start.3 = (bf16[8,352,768]{2,1,0:T(8,128)(2,1)S(1)}, bf16[8,352,768]{2,1,0:T(8,128)(2,1)}, u32[]{:S(2)}) copy-start(bf16[8,352,768]{2,1,0:T(8,128)(2,1)} %copy-done.2) | copy-start | bytes 12976132
  78.8 3.9 %copy-start = (bf16[1024,2816]{1,0:T(8,128)(2,1)}, bf16[1024,2816]{1,0:T(8,128)(2,1)S(1)}, u32[]{:S(2)}) copy-start(bf16[1024,2816]{1,0:T(8,128)(2,1)S(1)} %get-tuple-element.14.error_ref) | copy-start | bytes 17301508
  78.8 3.9 %copy-start.4 = (bf16[32,16,1664]{2,1,0:T(8,128)(2,1)}, bf16[32,16,1664]{2,1,0:T(8,128)(2,1)S(1)}, u32[]{:S(2)}) copy-start(bf16[32,16,1664]{2,1,0:T(8,128)(2,1)S(1)} %get-tuple-element.10) | copy-start | bytes 5111812
  82.7 10.9 %collective-permute-start = (bf16[1408,768]{1,0:T(8,128)(2,1)}, bf16[1408,768]{1,0:T(8,128)(2,1)}, u32[]{:S(2)}, u32[]{:S(2)}) collective-permute-start(bf16[1408,768]{1,0:T(8,128)(2,1)} %shard_map.80), channel_id=1, source_target_pairs={{0,32},{32,0},{64,96},{96,64},{128,160},{160,128},{192,224},{224,1... | collective-permute-start | bytes 6488072 | tf_op jit(solution)/shard_map/ppermute | solution.py:313
  82.7 48.3 %all-to-all-start.1 = ((bf16[32,16,1664]{2,1,0:T(8,128)(2,1)}), bf16[32,16,1664]{2,1,0:T(8,128)(2,1)S(1)}, u32[]{:S(2)}, u32[]{:S(2)}) async-start(bf16[32,16,1664]{2,1,0:T(8,128)(2,1)} %copy-done.4), calls=%async_computation.1 | async-start | bytes 3407872 | tf_op jit(solution)/shard_map/all_to_all | solution.py:291
  88.4 2.6 %copy-start.1 = (bf16[1024,2816]{1,0:T(8,128)(2,1)S(1)}, bf16[1024,2816]{1,0:T(8,128)(2,1)}, u32[]{:S(2)}) copy-start(bf16[1024,2816]{1,0:T(8,128)(2,1)} %copy-done) | copy-start | bytes 17301508
  95.3 35.6 %copy-start.6 = (bf16[1024,128]{1,0:T(8,128)(2,1)S(1)}, bf16[1024,128]{1,0:T(8,128)(2,1)}, u32[]{:S(2)}) copy-start(bf16[1024,128]{1,0:T(8,128)(2,1)} %copy-done.5) | copy-start | bytes 786436
  95.3 16.7 %collective-permute-start.1 = (bf16[352,768]{1,0:T(8,128)(2,1)S(1)}, bf16[352,768]{1,0:T(8,128)(2,1)S(1)}, u32[]{:S(2)}, u32[]{:S(2)}) collective-permute-start(bf16[352,768]{1,0:T(8,128)(2,1)S(1)} %get-tuple-element.15), channel_id=1, source_target_pairs={{0,128},{32,160},{64,192},{96,224},{128,0},{160,32},{192,64},{224,... | collective-permute-start | bytes 1622024 | tf_op jit(solution)/shard_map/ppermute | solution.py:323
  97.5 25.4 %collective-permute-start.3 = (bf16[352,768]{1,0:T(8,128)(2,1)S(1)}, bf16[352,768]{1,0:T(8,128)(2,1)S(1)}, u32[]{:S(2)}, u32[]{:S(2)}) collective-permute-start(bf16[352,768]{1,0:T(8,128)(2,1)S(1)} %get-tuple-element.16), channel_id=1, source_target_pairs={{0,192},{32,224},{64,0},{96,32},{128,64},{160,96},{192,128},{224,1... | collective-permute-start | bytes 1622024 | tf_op jit(solution)/shard_map/ppermute | solution.py:323
  99.0 24.0 %collective-permute-start.2 = (bf16[352,768]{1,0:T(8,128)(2,1)S(1)}, bf16[352,768]{1,0:T(8,128)(2,1)S(1)}, u32[]{:S(2)}, u32[]{:S(2)}) collective-permute-start(bf16[352,768]{1,0:T(8,128)(2,1)S(1)} %get-tuple-element.17), channel_id=1, source_target_pairs={{0,64},{32,96},{64,128},{96,160},{128,192},{160,224},{192,0},{224,... | collective-permute-start | bytes 1622024 | tf_op jit(solution)/shard_map/ppermute | solution.py:323

commit v3 on v2

--- a/solution.py
+++ b/solution.py
@@ -34,12 +34,20 @@
     return -(-block // 32) * 32
 
 
-def pack_kernel(labels, shards, shift_ref, embed_ref, short_ref, pos_ref, send_ref, pick_ref):
+def pack_kernel(labels, shards, embed_ref, short_ref, pos_ref, send_ref, pick_ref):
     rows, width = embed_ref.shape
     slots_k = short_ref.shape[0]
     clusters = send_ref.shape[0]
     cap = 2 * HALF
     block = labels // shards
+    place = lax.axis_index("rows")
+    core, x = lax.rem(place, 2), lax.div(place, 2)
+    half = shards // 2
+    shift = []
+    for b in range(shards):
+        step = lax.rem(b // 2 - x + half, half)
+        slot = step + jnp.where(core == b % 2, half, 0)
+        shift.append(padded(block) * slot - block * b)
     short = short_ref[...]
     pos = pos_ref[...]
     count = pos.shape[0]
@@ -58,9 +66,9 @@
     for j in range(slots_k):
         local = pos - j * labels
         inside = jnp.logical_and(local >= 0, local < labels)
-        column = local + shift_ref[0]
+        column = local + shift[0]
         for b in range(1, shards):
-            column += jnp.where(local >= b * block, shift_ref[b] - shift_ref[b - 1], 0)
+            column += jnp.where(local >= b * block, shift[b] - shift[b - 1], 0)
         column = jnp.where(inside, column, 0)
         bit = lax.shift_left(jnp.ones_like(column), lax.shift_right_logical(column, 7))
         values.append(jnp.where(inside, bit, 0).astype(F32))
@@ -115,15 +123,24 @@
 
 
 def score_kernel(
-    count, recv_ref, weight_ref, pads_ref, back_ref, error_out,
-    rows_ref, bits_ref, s_ref, error_ref, relu_ref, prod_ref, sum_ref, sem,
+    count, recv_ref, table_ref, pads_ref, back_out, give_out, keep_out,
+    weight_ref, back_ref, rows_ref, bits_ref, s_ref, error_ref, relu_ref, prod_ref, sum_ref,
+    weight_sem, error_sem, back_sem, rows_sem,
 ):
     sources = recv_ref.shape[0]
     total, width = rows_ref.shape
     chunks = weight_ref.shape[0] // CHUNK
+    loads = []
+    for i in range(chunks):
+        here = slice(i * CHUNK, (i + 1) * CHUNK)
+        load = pltpu.make_async_copy(table_ref.at[here], weight_ref.at[here], weight_sem.at[i])
+        load.start()
+        loads.append(load)
     assemble(recv_ref, rows_ref)
+    spare = pltpu.make_async_copy(rows_ref, give_out.at[:, keep_out.shape[1] :], rows_sem)
+    spare.start()
     target_bits(count, recv_ref, bits_ref, width)
-    copies = []
+    copies = [spare]
 
     def score(i, at):
         chunk = weight_ref[i * CHUNK : (i + 1) * CHUNK]
@@ -158,26 +175,28 @@
             prod_ref[here] = prod
             sum_ref[here] = summed
 
+    def flush(at):
+        half = keep_out.shape[1]
+        for k, out in enumerate((give_out, keep_out)):
+            copy = pltpu.make_async_copy(
+                error_ref.at[at, k * half : (k + 1) * half],
+                out.at[at, :half],
+                error_sem.at[2 * (at.start // BLOCK) + k],
+            )
+            copy.start()
+            copies.append(copy)
+
     blocks = [slice(k, k + BLOCK) for k in range(0, total, BLOCK)]
     for i in range(-1, chunks):
+        if i + 1 < chunks:
+            loads[i + 1].wait()
         for at in blocks:
             if i + 1 < chunks:
                 score(i + 1, at)
             if i >= 0:
                 pointwise(i, at)
-        if i >= 0:
-            columns = slice(i * CHUNK, (i + 1) * CHUNK)
-            copy = pltpu.make_async_copy(
-                error_ref.at[:, columns], error_out.at[:, columns], sem.at[i]
-            )
-            copy.start()
-            copies.append(copy)
     for at in blocks:
-        first, last = at.start // (2 * HALF), at.stop // (2 * HALF)
-        grads = dot(error_ref[at], weight_ref[...]).astype(BF)
-        grads = grads.reshape(last - first, 2 * HALF, width)
-        back_ref[first:last, :, :width] = grads[:, :HALF]
-        back_ref[first:last, :, width : 2 * width] = grads[:, HALF:]
+        flush(at)
 
     summed = sum_ref[...] - pads_ref[0:1]
     tail = jnp.where(summed < 4e-4, summed, jnp.log(prod_ref[...] * pads_ref[1:2]))
@@ -194,22 +213,82 @@
     mixed = jnp.where(side < 8, terms[:, HALF:], 0.0)
     mixed = jnp.where(side < 4, terms[:, :HALF], mixed)
     back_ref[:, :, 2 * width :] = mixed.astype(BF)
+    for at in blocks:
+        first, last = at.start // (2 * HALF), at.stop // (2 * HALF)
+        grads = dot(error_ref[at], weight_ref[...]).astype(BF)
+        grads = grads.reshape(last - first, 2 * HALF, width)
+        back_ref[first:last, :, :width] = grads[:, :HALF]
+        back_ref[first:last, :, width : 2 * width] = grads[:, HALF:]
+        copy = pltpu.make_async_copy(
+            back_ref.at[first:last], back_out.at[first:last], back_sem.at[at.start // BLOCK]
+        )
+        copy.start()
+        copies.append(copy)
     for copy in copies:
         copy.wait()
 
 
-def weight_kernel(error_ref, recv_ref, out_ref, rows_ref):
-    assemble(recv_ref, rows_ref)
-    labels = out_ref.shape[0]
-    for start in range(0, labels, 2 * CHUNK):
-        here = slice(start, min(start + 2 * CHUNK, labels))
-        out_ref[here] = dot(error_ref[:, here], rows_ref[...], TN).astype(out_ref.dtype)
-
-
-def combine_kernel(scale, got_ref, pick_ref, grad_ref, loss_ref):
+def weight_kernel(
+    mine_in, other_in, mine_rows, share_out, first_out, second_out, third_out,
+    mine_ref, other_ref, rows_ref, share_ref, parts_ref, load_sem, store_sem,
+):
+    half = mine_ref.shape[1]
+    middle = half // 2 // LANES * LANES
+    upper, lower = slice(middle, half), slice(0, middle)
+    loads = []
+    for source, target, here in (
+        (mine_in, mine_ref, upper),
+        (other_in, other_ref, slice(half, None)),
+        (other_in, other_ref, upper),
+        (mine_in, mine_ref, lower),
+        (other_in, other_ref, lower),
+    ):
+        load = pltpu.make_async_copy(
+            source.at[:, here], target.at[:, here], load_sem.at[len(loads)]
+        )
+        load.start()
+        loads.append(load)
+    assemble(mine_rows, rows_ref)
+    block = share_ref.shape[0]
+    stores = []
+    for i, (k, out) in enumerate(
+        ((2, second_out), (3, third_out), (1, first_out), (0, share_out))
+    ):
+        here = slice(k * block, (k + 1) * block)
+        if i in (0, 2):
+            loads[3 * (i // 2)].wait()
+        grads = dot(mine_ref[:, here], rows_ref[...], TN)
+        if i == 0:
+            loads[1].wait()
+            loads[2].wait()
+        if i == 2:
+            loads[4].wait()
+        grads += dot(other_ref[:, here], other_ref[:, half:], TN)
+        if k == 0:
+            share_ref[...] = grads
+            held = share_ref
+        else:
+            held = parts_ref.at[k - 1]
+            held[...] = grads.astype(BF)
+        store = pltpu.make_async_copy(held, out, store_sem.at[i])
+        store.start()
+        stores.append(store)
+    for store in stores:
+        store.wait()
+
+
+def combine_kernel(
+    scale, got_ref, pick_in, share_in, first_ref, second_ref, third_ref,
+    grad_ref, loss_ref, weight_ref, pick_ref, share_ref, sem,
+):
     clusters = got_ref.shape[0]
     width = grad_ref.shape[1]
     rows = grad_ref.shape[0]
+    loads = [pltpu.make_async_copy(pick_in, pick_ref, sem.at[0])]
+    loads.append(pltpu.make_async_copy(share_in, share_ref, sem.at[1]))
+    for load in loads:
+        load.start()
+    loads[0].wait()
     pick = pick_ref[...].reshape(clusters, 2 * HALF, rows)
     pick_a = pick[:, :HALF].reshape(clusters * HALF, rows)
     pick_b = pick[:, HALF:].reshape(clusters * HALF, rows)
@@ -224,6 +303,11 @@
     second = dot(terms, pick_b, TN)
     loss = jnp.sum(first[:4], axis=0, keepdims=True) + jnp.sum(second[4:8], axis=0, keepdims=True)
     loss_ref[...] = loss * scale
+    loads[1].wait()
+    total = share_ref[...]
+    for part in (first_ref, second_ref, third_ref):
+        total += part[...].astype(F32)
+    weight_ref[...] = total[: weight_ref.shape[0]].astype(BF)
 
 
 def whole(shape, dtype):
@@ -232,6 +316,13 @@
 
 VM = pl.BlockSpec(memory_space=pltpu.VMEM)
 SM = pl.BlockSpec(memory_space=pltpu.SMEM)
+HBM = pl.BlockSpec(memory_space=pltpu.HBM)
+
+
+def in_hbm(array):
+    return pltpu.with_memory_space_constraint(array, pltpu.HBM)
+
+
 PARAMS = pltpu.CompilerParams(vmem_limit_bytes=VMEM_LIMIT)
 
 
@@ -251,18 +342,14 @@
     place = lax.axis_index("rows")
     core, x = place % 2, place // 2
     order = [((x + k) % half) * 2 + side for side in (1 - core, core) for k in range(half)]
-    shard = jnp.arange(shards, dtype=jnp.int32)
-    step = (shard // 2 - x + half) % half
-    slot = jnp.where(shard % 2 == core, half + step, step)
-    shift = (tall * slot - block * shard).astype(jnp.int32)
 
     send, pick = pl.pallas_call(
         functools.partial(pack_kernel, labels, shards),
         out_shape=(whole((clusters, HALF, wide), BF), whole((total, rows), BF)),
-        in_specs=[SM] + [VM] * 3,
+        in_specs=[VM] * 3,
         out_specs=(VM, VM),
-        compiler_params=PARAMS,
-    )(shift, embed, shortlist.T, positives.T)
+        compiler_params=pltpu.CompilerParams(vmem_limit_bytes=60 * 1024 * 1024),
+    )(embed, shortlist.T, positives.T)
     recv = lax.all_to_all(send, "clus", 0, 0, tiled=True)
 
     table = jnp.pad(weights.reshape(shards, block, width), ((0, 0), (0, tall - block), (0, 0)))
@@ -271,12 +358,18 @@
     column = np.arange(shards * tall)
     pads = np.bincount(column[column % tall >= block] % LANES, minlength=LANES)
     pads = np.stack([pads, 0.5**pads]).astype(np.float32)
-    back, error = pl.pallas_call(
+    back, give, keep = pl.pallas_call(
         functools.partial(score_kernel, count),
-        out_shape=(whole((clusters, HALF, wide), BF), whole((total, shards * tall), BF)),
-        in_specs=[VM, VM, VM],
-        out_specs=(VM, pl.BlockSpec(memory_space=pl.ANY)),
+        out_shape=(
+            pltpu.HBM((clusters, HALF, wide), BF),
+            pltpu.HBM((total, half * tall + width), BF),
+            pltpu.HBM((total, half * tall), BF),
+        ),
+        in_specs=[VM, HBM, VM],
+        out_specs=(HBM, HBM, HBM),
         scratch_shapes=[
+            pltpu.VMEM((shards * tall, width), BF),
+            pltpu.VMEM((clusters, HALF, wide), BF),
             pltpu.VMEM((total, width), BF),
             pltpu.VMEM((total, LANES), jnp.int32),
             pltpu.VMEM((2, total, CHUNK), F32),
@@ -285,56 +378,51 @@
             pltpu.VMEM((total, LANES), F32),
             pltpu.VMEM((total, LANES), F32),
             pltpu.SemaphoreType.DMA((shards * tall // CHUNK,)),
+            pltpu.SemaphoreType.DMA((2 * total // BLOCK,)),
+            pltpu.SemaphoreType.DMA((total // BLOCK,)),
+            pltpu.SemaphoreType.DMA,
         ],
         compiler_params=PARAMS,
-    )(recv, table, jnp.asarray(pads))
+    )(recv, in_hbm(table), jnp.asarray(pads))
     got = lax.all_to_all(back, "clus", 0, 0, tiled=True)
 
-    def weight_part(index, dtype):
-        size = half * tall
-        work = total * size * width
-        return pl.pallas_call(
-            weight_kernel,
-            grid=(1,),
-            out_shape=whole((size, width), dtype),
-            in_specs=[
-                pl.BlockSpec((total, size), lambda i: (0, index)),
-                pl.BlockSpec((clusters, HALF, wide), lambda i: (0, 0, 0)),
-            ],
-            out_specs=pl.BlockSpec((size, width), lambda i: (0, 0)),
-            scratch_shapes=[pltpu.VMEM((total, width), BF)],
-            compiler_params=PARAMS,
-            cost_estimate=pl.CostEstimate(
-                flops=2 * work, bytes_accessed=8 * 1024 * 1024, transcendentals=0
-            ),
-        )(error, recv)
-
-    give = weight_part(0, BF)
-    taken = lax.ppermute(give, "rows", [(i, i ^ 1) for i in range(shards)])
-    keep = weight_part(1, F32)
-
-    def piece(k):
-        here = slice(k * tall, (k + 1) * tall)
-        return keep[here] + taken[here].astype(F32)
-
+    swap = [(i, i ^ 1) for i in range(shards)]
+    other = lax.ppermute(give, "rows", swap)
+    share, *pieces = pl.pallas_call(
+        weight_kernel,
+        out_shape=(pltpu.HBM((tall, width), F32),) + (pltpu.HBM((tall, width), BF),) * 3,
+        in_specs=[HBM, HBM, VM],
+        out_specs=(HBM,) * 4,
+        scratch_shapes=[
+            pltpu.VMEM((total, half * tall), BF),
+            pltpu.VMEM((total, half * tall + width), BF),
+            pltpu.VMEM((total, width), BF),
+            pltpu.VMEM((tall, width), F32),
+            pltpu.VMEM((half - 1, tall, width), BF),
+            pltpu.SemaphoreType.DMA((5,)),
+            pltpu.SemaphoreType.DMA((4,)),
+        ],
+        compiler_params=PARAMS,
+        cost_estimate=pl.CostEstimate(flops=1, bytes_accessed=1, transcendentals=0),
+    )(in_hbm(keep), in_hbm(other), recv)
     arrived = []
     for k in (2, 1, 3):
         perm = [(i, (i + 2 * k) % shards) for i in range(shards)]
-        arrived.append(lax.ppermute(piece(k).astype(BF), "rows", perm))
-    share = piece(0)
-
-    row_grad, row_loss = pl.pallas_call(
+        arrived.append(lax.ppermute(pieces[k - 1], "rows", perm))
+
+    row_grad, row_loss, weight_grad = pl.pallas_call(
         functools.partial(combine_kernel, 1.0 / (slots_k * labels)),
-        out_shape=(whole((rows, width), BF), whole((1, rows), F32)),
-        in_specs=[VM] * 2,
-        out_specs=(VM, VM),
+        out_shape=(whole((rows, width), BF), whole((1, rows), F32), whole((block, width), BF)),
+        in_specs=[VM, HBM, HBM, VM, VM, VM],
+        out_specs=(VM, VM, VM),
+        scratch_shapes=[
+            pltpu.VMEM((total, rows), BF),
+            pltpu.VMEM((tall, width), F32),
+            pltpu.SemaphoreType.DMA((2,)),
+        ],
         compiler_params=PARAMS,
-    )(got, pick)
-
-    for part in arrived:
-        share = share + part.astype(F32)
-    weight_grad = share[:block].astype(BF)[None]
-    return row_grad, row_loss.reshape(rows), weight_grad
+    )(got, in_hbm(pick), in_hbm(share), *arrived)
+    return row_grad, row_loss.reshape(rows), weight_grad[None]
 
 
 def solution(mesh):

time: 133 us -> 126 us (0.947)
  Pallas kernels: 26.9 us -> 33 us
  local copies, waits for them, and re-layouts: 17.7 us -> 12.6 us
  waiting for transfers between devices: 62.2 us -> 57.3 us
  other arithmetic: 2.94 us -> 0 us
    ppermute x4, waiting for transfers between devices: 22.4 us -> 2.07 us  [the longest x1 2.06 us: local(): other = lax.ppermute(give, 'rows', swap)]
    all_to_all x1, waiting for transfers between devices: 6.8 us -> 26 us  [local(): got = lax.all_to_all(back, 'clus', 0, 0, tiled=True)]
    unnamed x31 -> x11, local copies, waits for them, and re-layouts: 12.5 us -> 7.64 us
    pallas_call x3 -> x2, Pallas kernels: 23 us -> 27.3 us  [the longest x1 17.1 us: local(): pl.pallas_call(functools.partial(score_kernel, count), out_shape=(pltpu.H...]
    all_to_all x1, waiting for transfers between devices: 33.1 us -> 29.3 us  [local(): recv = lax.all_to_all(send, 'clus', 0, 0, tiled=True)]
    convert_element_type x1 -> x0, other arithmetic: 1.79 us -> none  [local(): arrived.append(lax.ppermute(piece(k).astype(BF), 'rows', perm))]
  transfers between devices with their start and end apart: 6 -> 6, of which waited for: 5 -> 3; matrix products, arithmetic and copies ran while one was open for 7% -> 10% of each run, Pallas kernels for 2% -> 8%
where the time goes in v3:
time: 126 us; the launch traced here: 125 us
  waiting for transfers between devices  57.3 us (45%)
  Pallas kernels  33 us (26%)
  starting transfers between devices  21.6 us (17%)
  local copies, waits for them, and re-layouts  12.6 us (10%)
    all_to_all x1, waiting for transfers between devices, local(): recv = lax.all_to_all(send, 'clus', 0, 0, tiled=True)  29.3 us
    all_to_all x1, waiting for transfers between devices, local(): got = lax.all_to_all(back, 'clus', 0, 0, tiled=True)  26 us
    pallas_call x1, Pallas kernels, local(): pl.pallas_call(functools.partial(score_kernel, count), out_shape=(pltpu.H...  17.1 us
    all_to_all x1, starting transfers between devices, local(): recv = lax.all_to_all(send, 'clus', 0, 0, tiled=True)  11.5 us
    pallas_call x1, Pallas kernels, local(): pl.pallas_call(weight_kernel, out_shape=(pltpu.HBM((tall, width), F32),)...  10.2 us
    unnamed x11, local copies, waits for them, and re-layouts  7.64 us
    all_to_all x1, starting transfers between devices, local(): got = lax.all_to_all(back, 'clus', 0, 0, tiled=True)  5.79 us
    ppermute x3, starting transfers between devices, local(): arrived.append(lax.ppermute(pieces[k - 1], 'rows', perm))  4.27 us
  transfers between devices with their start and end apart: 6, of which 3 were waited for; matrix products, arithmetic and copies ran while one was open for 10% of the time, Pallas kernels for 8%

profile of v3, /device:TPU:2, one launch (start us, length us, event | category | flops | bytes accessed | tf_op | source)
XLA Modules:
  0.0 125.5 jit_solution(10014339298189952873)
XLA Ops:
  0.6 3.2 %shard_map.76 = (bf16[32,16,1664]{2,1,0:T(8,128)(2,1)}, bf16[1024,128]{1,0:T(8,128)(2,1)}) custom-call(bf16[128,768]{1,0:T(8,128)(2,1)} %embed_ref.1, s32[4,128]{1,0:T(4,128)} %bitcast.6, s32[8,128]{1,0:T(8,128)} %bitcast.5), custom_call_target="tpu_custom_call" | custom-call | tf_op jit(solution)/shard_map/pallas_call | solution.py:346
  3.8 11.5 %all-to-all-start = ((bf16[32,16,1664]{2,1,0:T(8,128)(2,1)}), bf16[32,16,1664]{2,1,0:T(8,128)(2,1)S(1)}, u32[]{:S(2)}, u32[]{:S(2)}) async-start(bf16[32,16,1664]{2,1,0:T(8,128)(2,1)} %get-tuple-element.15), calls=%async_computation | async-start | bytes 3407872 | tf_op jit(solution)/shard_map/all_to_all | solution.py:353
  15.4 4.2 %reshape.15 = bf16[8,342,768]{2,1,0:T(8,128)(2,1)} reshape(bf16[1,2736,768]{2,1,0:T(8,128)(2,1)} %param.6) | data formatting | bytes 8404992 | tf_op jit(solution)/shard_map/reshape | solution.py:355
  19.6 2.0 %fusion = bf16[8,352,768]{2,1,0:T(8,128)(2,1)} fusion(s32[]{:T(128)S(6)} %select_n.63, bf16[8,342,768]{2,1,0:T(8,128)(2,1)} %reshape.15), kind=kLoop, calls=%fused_computation.8 | loop fusion | bytes 4743172
  21.6 0.5 copy-done.1
  22.1 0.8 fusion.1
  23.0 0.9 fusion.2
  23.8 0.9 fusion.3
  24.7 0.9 fusion.4
  25.5 0.8 fusion.5
  26.4 0.8 fusion.6
  27.2 0.8 fusion.7
  28.0 29.3 %all-to-all-done.recv_ref.mine_rows = bf16[32,16,1664]{2,1,0:T(8,128)(2,1)S(1)} async-done(((bf16[32,16,1664]{2,1,0:T(8,128)(2,1)}), bf16[32,16,1664]{2,1,0:T(8,128)(2,1)S(1)}, u32[]{:S(2)}, u32[]{:S(2)}) %all-to-all-start) | async-done | bytes 1703968 | tf_op jit(solution)/shard_map/all_to_all | solution.py:353
  57.3 17.1 %shard_map.77 = (bf16[32,16,1664]{2,1,0:T(8,128)(2,1)}, bf16[1024,2176]{1,0:T(8,128)(2,1)}, bf16[1024,1408]{1,0:T(8,128)(2,1)}) custom-call(bf16[32,16,1664]{2,1,0:T(8,128)(2,1)S(1)} %all-to-all-done.recv_ref.mine_rows, bf16[2816,768]{1,0:T(8,128)(2,1)} %bitcast.2.table_ref, f32[2,128]{1,0:T(2,128)S(1)} %copy-done), custom_call_target="tpu_custom_call" | custom-call | tf_op jit(solution)/shard_map/pallas_call | solution.py:361
  74.4 0.1 collective-permute-start
  74.5 5.8 %all-to-all-start.1 = ((bf16[32,16,1664]{2,1,0:T(8,128)(2,1)}), bf16[32,16,1664]{2,1,0:T(8,128)(2,1)S(1)}, u32[]{:S(2)}, u32[]{:S(2)}) async-start(bf16[32,16,1664]{2,1,0:T(8,128)(2,1)} %get-tuple-element.16), calls=%async_computation.1 | async-start | bytes 3407872 | tf_op jit(solution)/shard_map/all_to_all | solution.py:387
  80.3 2.1 %collective-permute-done.other_in = bf16[1024,2176]{1,0:T(8,128)(2,1)} collective-permute-done((bf16[1024,2176]{1,0:T(8,128)(2,1)}, bf16[1024,2176]{1,0:T(8,128)(2,1)}, u32[]{:S(2)}, u32[]{:S(2)}) %collective-permute-start) | collective-permute-done | bytes 4456480 | tf_op jit(solution)/shard_map/ppermute | solution.py:390
  82.4 10.2 %shard_map.78 = (f32[352,768]{1,0:T(8,128)}, bf16[352,768]{1,0:T(8,128)(2,1)}, bf16[352,768]{1,0:T(8,128)(2,1)}, bf16[352,768]{1,0:T(8,128)(2,1)}) custom-call(bf16[1024,1408]{1,0:T(8,128)(2,1)} %get-tuple-element.18.mine_in, bf16[1024,2176]{1,0:T(8,128)(2,1)} %collective-permute-done.other_in, bf16[32,16,1664]{2,1,0:T(8,128)(2,1)S(1)} %all-to-all-done.recv_ref.mine_rows), custom_call_target="tpu_custom_call" | custom-call | flops 1 | bytes 1 | tf_op jit(solution)/shard_map/pallas_call | solution.py:391
  92.6 2.2 %collective-permute-start.1 = (bf16[352,768]{1,0:T(8,128)(2,1)}, bf16[352,768]{1,0:T(8,128)(2,1)S(1)}, u32[]{:S(2)}, u32[]{:S(2)}) collective-permute-start(bf16[352,768]{1,0:T(8,128)(2,1)} %get-tuple-element.21), channel_id=1, source_target_pairs={{0,128},{32,160},{64,192},{96,224},{128,0},{160,32},{192,64},{224,... | collective-permute-start | bytes 1622024 | tf_op jit(solution)/shard_map/ppermute | solution.py:411
  94.9 0.0 collective-permute-start.2
  94.9 2.0 %collective-permute-start.3 = (bf16[352,768]{1,0:T(8,128)(2,1)}, bf16[352,768]{1,0:T(8,128)(2,1)S(1)}, u32[]{:S(2)}, u32[]{:S(2)}) collective-permute-start(bf16[352,768]{1,0:T(8,128)(2,1)} %get-tuple-element.23), channel_id=1, source_target_pairs={{0,192},{32,224},{64,0},{96,32},{128,64},{160,96},{192,128},{224,1... | collective-permute-start | bytes 1622024 | tf_op jit(solution)/shard_map/ppermute | solution.py:411
  96.9 26.0 %all-to-all-done.1.got_ref = bf16[32,16,1664]{2,1,0:T(8,128)(2,1)S(1)} async-done(((bf16[32,16,1664]{2,1,0:T(8,128)(2,1)}), bf16[32,16,1664]{2,1,0:T(8,128)(2,1)S(1)}, u32[]{:S(2)}, u32[]{:S(2)}) %all-to-all-start.1) | async-done | bytes 1703968 | tf_op jit(solution)/shard_map/all_to_all | solution.py:387
  122.8 0.0 collective-permute-done.1.first_ref
  122.9 2.5 %shard_map.79 = (bf16[128,768]{1,0:T(8,128)(2,1)}, f32[1,128]{1,0:T(1,128)}, bf16[342,768]{1,0:T(8,128)(2,1)}) custom-call(bf16[32,16,1664]{2,1,0:T(8,128)(2,1)S(1)} %all-to-all-done.1.got_ref, bf16[1024,128]{1,0:T(8,128)(2,1)} %get-tuple-element.17.pick_in, f32[352,768]{1,0:T(8,128)} %get-tuple-element.20.share_in, ...), custom_call_target="tpu_custom_call" | custom-call | tf_op jit(solution)/shard_map/pallas_call | solution.py:413
  (5 shorter events, 0.0 us)
Async XLA Ops:
  3.8 53.5 %all-to-all-start = ((bf16[32,16,1664]{2,1,0:T(8,128)(2,1)}), bf16[32,16,1664]{2,1,0:T(8,128)(2,1)S(1)}, u32[]{:S(2)}, u32[]{:S(2)}) async-start(bf16[32,16,1664]{2,1,0:T(8,128)(2,1)} %get-tuple-element.15), calls=%async_computation | async-start | bytes 3407872 | tf_op jit(solution)/shard_map/all_to_all | solution.py:353
  19.6 2.6 %copy-start.1 = (bf16[8,342,768]{2,1,0:T(8,128)(2,1)S(1)}, bf16[8,342,768]{2,1,0:T(8,128)(2,1)}, u32[]{:S(2)}) copy-start(bf16[8,342,768]{2,1,0:T(8,128)(2,1)} %reshape.15) | copy-start | bytes 12607492
  26.4 30.9 %copy-start = (f32[2,128]{1,0:T(2,128)S(1)}, f32[2,128]{1,0:T(2,128)}, u32[]{:S(2)}) copy-start(f32[2,128]{1,0:T(2,128)} %constant.86.clone.pads_ref) | copy-start | bytes 3076
  74.4 8.0 %collective-permute-start = (bf16[1024,2176]{1,0:T(8,128)(2,1)}, bf16[1024,2176]{1,0:T(8,128)(2,1)}, u32[]{:S(2)}, u32[]{:S(2)}) collective-permute-start(bf16[1024,2176]{1,0:T(8,128)(2,1)} %get-tuple-element.19), channel_id=1, source_target_pairs={{0,32},{32,0},{64,96},{96,64},{128,160},{160,128},{192,224},{224,1... | collective-permute-start | bytes 13369352 | tf_op jit(solution)/shard_map/ppermute | solution.py:390
  74.5 48.4 %all-to-all-start.1 = ((bf16[32,16,1664]{2,1,0:T(8,128)(2,1)}), bf16[32,16,1664]{2,1,0:T(8,128)(2,1)S(1)}, u32[]{:S(2)}, u32[]{:S(2)}) async-start(bf16[32,16,1664]{2,1,0:T(8,128)(2,1)} %get-tuple-element.16), calls=%async_computation.1 | async-start | bytes 3407872 | tf_op jit(solution)/shard_map/all_to_all | solution.py:387
  92.6 30.2 %collective-permute-start.1 = (bf16[352,768]{1,0:T(8,128)(2,1)}, bf16[352,768]{1,0:T(8,128)(2,1)S(1)}, u32[]{:S(2)}, u32[]{:S(2)}) collective-permute-start(bf16[352,768]{1,0:T(8,128)(2,1)} %get-tuple-element.21), channel_id=1, source_target_pairs={{0,128},{32,160},{64,192},{96,224},{128,0},{160,32},{192,64},{224,... | collective-permute-start | bytes 1622024 | tf_op jit(solution)/shard_map/ppermute | solution.py:411
  94.9 28.0 %collective-permute-start.2 = (bf16[352,768]{1,0:T(8,128)(2,1)}, bf16[352,768]{1,0:T(8,128)(2,1)S(1)}, u32[]{:S(2)}, u32[]{:S(2)}) collective-permute-start(bf16[352,768]{1,0:T(8,128)(2,1)} %get-tuple-element.22), channel_id=1, source_target_pairs={{0,64},{32,96},{64,128},{96,160},{128,192},{160,224},{192,0},{224,... | collective-permute-start | bytes 1622024 | tf_op jit(solution)/shard_map/ppermute | solution.py:411
  94.9 28.0 %collective-permute-start.3 = (bf16[352,768]{1,0:T(8,128)(2,1)}, bf16[352,768]{1,0:T(8,128)(2,1)S(1)}, u32[]{:S(2)}, u32[]{:S(2)}) collective-permute-start(bf16[352,768]{1,0:T(8,128)(2,1)} %get-tuple-element.23), channel_id=1, source_target_pairs={{0,192},{32,224},{64,0},{96,32},{128,64},{160,96},{192,128},{224,1... | collective-permute-start | bytes 1622024 | tf_op jit(solution)/shard_map/ppermute | solution.py:411

commit v4 on v3

--- a/solution.py
+++ b/solution.py
@@ -11,7 +11,9 @@
 F32 = jnp.float32
 LANES = 128
 CHUNK = 256
-HALF = 16
+CAP = 32
+GROUP = 8
+GROUP_LANES = 32
 VMEM_LIMIT = 40 * 1024 * 1024
 TALL = 32
 BLOCK = 512
@@ -34,11 +36,13 @@
     return -(-block // 32) * 32
 
 
-def pack_kernel(labels, shards, embed_ref, short_ref, pos_ref, send_ref, pick_ref):
+def pack_kernel(
+    labels, shards, embed_ref, short_ref, pos_ref, send_out, pick_ref, held_ref, sem
+):
     rows, width = embed_ref.shape
     slots_k = short_ref.shape[0]
-    clusters = send_ref.shape[0]
-    cap = 2 * HALF
+    clusters = send_out.shape[0]
+    cap = CAP
     block = labels // shards
     place = lax.axis_index("rows")
     core, x = lax.rem(place, 2), lax.div(place, 2)
@@ -81,45 +85,59 @@
     got_values = dot(pick, values, NT)
     got_names = dot(pick, names, NT)
     own = lax.shift_right_logical(iota(got_values.shape, 0), 5).astype(F32)
-    kept = jnp.where(got_names == own, got_values, 0.0).astype(BF)
-    kept = kept.reshape(clusters, cap, LANES)
+    kept = jnp.where(got_names == own, got_values, 0.0)
+    kept = kept.reshape(clusters, cap // GROUP, GROUP, LANES)
     source = iota((LANES, LANES), 0)
+    folded = jnp.bitwise_and(source, 2 * count - 1)
+    folded = jnp.where(source < used, folded, LANES)
     target = iota((LANES, LANES), 1)
-    folded = jnp.bitwise_and(source, 2 * count - 1)
-    valid = source < used
-    fold_a = jnp.logical_and(valid, folded == target).astype(BF)
-    fold_b = jnp.logical_and(valid, folded + 2 * count == target).astype(BF)
-    meta = dot(kept[:, :HALF].reshape(clusters * HALF, LANES), fold_a)
-    meta += dot(kept[:, HALF:].reshape(clusters * HALF, LANES), fold_b)
-    got = dot(pick, embed_ref[...]).astype(BF).reshape(clusters, cap, width)
-    send_ref[:, :, :width] = got[:, :HALF]
-    send_ref[:, :, width : 2 * width] = got[:, HALF:]
-    send_ref[:, :, 2 * width :] = meta.astype(BF).reshape(clusters, HALF, LANES)
+    meta = jnp.zeros((clusters * GROUP, LANES), F32)
+    for g in range(cap // GROUP):
+        fold = (folded + g * GROUP_LANES == target).astype(BF)
+        part = kept[:, g].reshape(clusters * GROUP, LANES).astype(BF)
+        meta += dot(part, fold)
+    held_ref[:, width // LANES * cap :, :] = meta.astype(BF).reshape(clusters, GROUP, LANES)
+    step = clusters // 4
+    copies = []
+    for i in range(4):
+        here = slice(i * step, (i + 1) * step)
+        got = dot(pick[i * step * cap : (i + 1) * step * cap], embed_ref[...]).astype(BF)
+        for k in range(width // LANES):
+            part = got[:, k * LANES : (k + 1) * LANES]
+            held_ref[here, k * cap : (k + 1) * cap, :] = part.reshape(step, cap, LANES)
+        copy = pltpu.make_async_copy(held_ref.at[here], send_out.at[here], sem.at[i])
+        copy.start()
+        copies.append(copy)
+    for copy in copies:
+        copy.wait()
 
 
 def assemble(recv_ref, rows_ref):
     total, width = rows_ref.shape
-    left, right = recv_ref[:, :, :width], recv_ref[:, :, width : 2 * width]
-    rows_ref[...] = jnp.concatenate([left, right], axis=1).reshape(total, width)
+    for k in range(width // LANES):
+        part = recv_ref[:, k * CAP : (k + 1) * CAP, :]
+        rows_ref[:, k * LANES : (k + 1) * LANES] = part.reshape(total, LANES)
 
 
 def target_bits(count, recv_ref, bits_ref, width):
     sources = recv_ref.shape[0]
     step = 8
+    tall = step * GROUP
     for start in range(0, sources, step):
-        meta = recv_ref[start : start + step, :, 2 * width :].astype(F32).astype(jnp.int32)
-        meta = meta.reshape(step * HALF, LANES)
-        lane = iota((step * HALF, LANES), 1)
-        halves = []
-        for base in (0, 2 * count):
-            bits = jnp.zeros((step * HALF, LANES), jnp.int32)
+        meta = recv_ref[start : start + step, width // LANES * CAP :, :]
+        meta = meta.astype(F32).astype(jnp.int32).reshape(tall, LANES)
+        lane = iota((tall, LANES), 1)
+        groups = []
+        for g in range(CAP // GROUP):
+            base = g * GROUP_LANES
+            bits = jnp.zeros((tall, LANES), jnp.int32)
             for p in range(count):
                 value = meta[:, base + p : base + p + 1]
                 place = meta[:, base + count + p : base + count + p + 1]
                 bits = jnp.bitwise_or(bits, jnp.where(place == lane, value, 0))
-            halves.append(bits.reshape(step, HALF, LANES))
-        both = jnp.concatenate(halves, axis=1)
-        bits_ref[start * 2 * HALF : (start + step) * 2 * HALF] = both.reshape(-1, LANES)
+            groups.append(bits.reshape(step, GROUP, LANES))
+        both = jnp.concatenate(groups, axis=1)
+        bits_ref[start * CAP : (start + step) * CAP] = both.reshape(step * CAP, LANES)
 
 
 def score_kernel(
@@ -208,17 +226,18 @@
     terms = jnp.where(part == 2, third, 0.0)
     terms = jnp.where(part == 1, second, terms)
     terms = jnp.where(part == 0, first, terms)
-    terms = terms.reshape(sources, 2 * HALF, LANES)
-    side = iota((sources, HALF, LANES), 2)
-    mixed = jnp.where(side < 8, terms[:, HALF:], 0.0)
-    mixed = jnp.where(side < 4, terms[:, :HALF], mixed)
-    back_ref[:, :, 2 * width :] = mixed.astype(BF)
+    terms = terms.reshape(sources, CAP // GROUP, GROUP, LANES)
+    group = lax.shift_right_logical(iota((sources, GROUP, LANES), 2), 2)
+    mixed = jnp.zeros((sources, GROUP, LANES), F32)
+    for g in range(CAP // GROUP):
+        mixed = jnp.where(group == g, terms[:, g], mixed)
+    back_ref[:, width // LANES * CAP :, :] = mixed.astype(BF)
     for at in blocks:
-        first, last = at.start // (2 * HALF), at.stop // (2 * HALF)
+        first, last = at.start // CAP, at.stop // CAP
         grads = dot(error_ref[at], weight_ref[...]).astype(BF)
-        grads = grads.reshape(last - first, 2 * HALF, width)
-        back_ref[first:last, :, :width] = grads[:, :HALF]
-        back_ref[first:last, :, width : 2 * width] = grads[:, HALF:]
+        for k in range(width // LANES):
+            part = grads[:, k * LANES : (k + 1) * LANES]
+            back_ref[first:last, k * CAP : (k + 1) * CAP, :] = part.reshape(last - first, CAP, LANES)
         copy = pltpu.make_async_copy(
             back_ref.at[first:last], back_out.at[first:last], back_sem.at[at.start // BLOCK]
         )
@@ -288,26 +307,26 @@
     loads.append(pltpu.make_async_copy(share_in, share_ref, sem.at[1]))
     for load in loads:
         load.start()
+    loads[1].wait()
+    summed = share_ref[...]
+    for part in (first_ref, second_ref, third_ref):
+        summed += part[...].astype(F32)
+    weight_ref[...] = summed[: weight_ref.shape[0]].astype(BF)
     loads[0].wait()
-    pick = pick_ref[...].reshape(clusters, 2 * HALF, rows)
-    pick_a = pick[:, :HALF].reshape(clusters * HALF, rows)
-    pick_b = pick[:, HALF:].reshape(clusters * HALF, rows)
-
-    def lanes(start, size):
-        return got_ref[:, :, start : start + size].reshape(clusters * HALF, size)
-
-    grads = dot(pick_a, lanes(0, width), TN) + dot(pick_b, lanes(width, width), TN)
+    parts = []
+    for k in range(width // LANES):
+        part = got_ref[:, k * CAP : (k + 1) * CAP, :]
+        parts.append(part.reshape(clusters * CAP, LANES))
+    grads = dot(pick_ref[...], jnp.concatenate(parts, axis=1), TN)
     grad_ref[...] = grads.astype(BF)
-    terms = lanes(2 * width, LANES)
-    first = dot(terms, pick_a, TN)
-    second = dot(terms, pick_b, TN)
-    loss = jnp.sum(first[:4], axis=0, keepdims=True) + jnp.sum(second[4:8], axis=0, keepdims=True)
+    terms = got_ref[:, width // LANES * CAP :, :].reshape(clusters * GROUP, LANES)
+    pick = pick_ref[...].astype(F32).reshape(clusters, CAP // GROUP, GROUP, rows)
+    loss = jnp.zeros((1, rows), F32)
+    for g in range(CAP // GROUP):
+        chosen = pick[:, g].reshape(clusters * GROUP, rows).astype(BF)
+        found = dot(terms, chosen, TN)
+        loss += jnp.sum(found[4 * g : 4 * g + 4], axis=0, keepdims=True)
     loss_ref[...] = loss * scale
-    loads[1].wait()
-    total = share_ref[...]
-    for part in (first_ref, second_ref, third_ref):
-        total += part[...].astype(F32)
-    weight_ref[...] = total[: weight_ref.shape[0]].astype(BF)
 
 
 def whole(shape, dtype):
@@ -333,8 +352,8 @@
     _, labels, _ = weights.shape
     clusters = lax.axis_size("clus")
     shards = lax.axis_size("rows")
-    wide = 2 * width + LANES
-    total = clusters * 2 * HALF
+    shape = (clusters, width // LANES * CAP + GROUP, LANES)
+    total = clusters * CAP
     block = labels // shards
     tall = padded(block)
     half = shards // 2
@@ -345,9 +364,10 @@
 
     send, pick = pl.pallas_call(
         functools.partial(pack_kernel, labels, shards),
-        out_shape=(whole((clusters, HALF, wide), BF), whole((total, rows), BF)),
+        out_shape=(pltpu.HBM(shape, BF), whole((total, rows), BF)),
         in_specs=[VM] * 3,
-        out_specs=(VM, VM),
+        out_specs=(HBM, VM),
+        scratch_shapes=[pltpu.VMEM(shape, BF), pltpu.SemaphoreType.DMA((4,))],
         compiler_params=pltpu.CompilerParams(vmem_limit_bytes=60 * 1024 * 1024),
     )(embed, shortlist.T, positives.T)
     recv = lax.all_to_all(send, "clus", 0, 0, tiled=True)
@@ -361,7 +381,7 @@
     back, give, keep = pl.pallas_call(
         functools.partial(score_kernel, count),
         out_shape=(
-            pltpu.HBM((clusters, HALF, wide), BF),
+            pltpu.HBM(shape, BF),
             pltpu.HBM((total, half * tall + width), BF),
             pltpu.HBM((total, half * tall), BF),
         ),
@@ -369,7 +389,7 @@
         out_specs=(HBM, HBM, HBM),
         scratch_shapes=[
             pltpu.VMEM((shards * tall, width), BF),
-            pltpu.VMEM((clusters, HALF, wide), BF),
+            pltpu.VMEM(shape, BF),
             pltpu.VMEM((total, width), BF),
             pltpu.VMEM((total, LANES), jnp.int32),
             pltpu.VMEM((2, total, CHUNK), F32),

time: 126 us -> 124 us (0.984)
  waiting for transfers between devices: 57.3 us -> 54.6 us
  Pallas kernels: 33 us -> 34.3 us
    all_to_all x1, waiting for transfers between devices: 26 us -> 24.5 us  [local(): got = lax.all_to_all(back, 'clus', 0, 0, tiled=True)]
    all_to_all x1, waiting for transfers between devices: 29.3 us -> 27.9 us  [local(): recv = lax.all_to_all(send, 'clus', 0, 0, tiled=True)]
where the time goes in v4:
time: 124 us
  waiting for transfers between devices  54.6 us (44%)
  Pallas kernels  34.3 us (28%)
  starting transfers between devices  21.5 us (17%)
  local copies, waits for them, and re-layouts  12.6 us (10%)
    all_to_all x1, waiting for transfers between devices, local(): recv = lax.all_to_all(send, 'clus', 0, 0, tiled=True)  27.9 us
    all_to_all x1, waiting for transfers between devices, local(): got = lax.all_to_all(back, 'clus', 0, 0, tiled=True)  24.5 us
    pallas_call x1, Pallas kernels, local(): pl.pallas_call(functools.partial(score_kernel, count), out_shape=(pltpu.H...  17.4 us
    all_to_all x1, starting transfers between devices, local(): recv = lax.all_to_all(send, 'clus', 0, 0, tiled=True)  11.5 us
    pallas_call x1, Pallas kernels, local(): pl.pallas_call(weight_kernel, out_shape=(pltpu.HBM((tall, width), F32),)...  10.3 us
    unnamed x11, local copies, waits for them, and re-layouts  7.64 us
    all_to_all x1, starting transfers between devices, local(): got = lax.all_to_all(back, 'clus', 0, 0, tiled=True)  5.71 us
    ppermute x3, starting transfers between devices, local(): arrived.append(lax.ppermute(pieces[k - 1], 'rows', perm))  4.23 us
  transfers between devices with their start and end apart: 6, of which 3 were waited for; matrix products, arithmetic and copies ran while one was open for 10% of the time, Pallas kernels for 8%

profile of v4, /device:TPU:2, one launch (start us, length us, event | category | flops | bytes accessed | tf_op | source)
XLA Modules:
  0.0 123.9 jit_solution(11891164687744225819)
XLA Ops:
  0.6 3.6 %shard_map.76 = (bf16[32,200,128]{2,1,0:T(8,128)(2,1)}, bf16[1024,128]{1,0:T(8,128)(2,1)}) custom-call(bf16[128,768]{1,0:T(8,128)(2,1)} %embed_ref.1, s32[4,128]{1,0:T(4,128)} %bitcast.6, s32[8,128]{1,0:T(8,128)} %bitcast.5), custom_call_target="tpu_custom_call" | custom-call | tf_op jit(solution)/shard_map/pallas_call | solution.py:365
  4.3 11.5 %all-to-all-start = ((bf16[32,200,128]{2,1,0:T(8,128)(2,1)}), bf16[32,200,128]{2,1,0:T(8,128)(2,1)S(1)}, u32[]{:S(2)}, u32[]{:S(2)}) async-start(bf16[32,200,128]{2,1,0:T(8,128)(2,1)} %get-tuple-element.15), calls=%async_computation | async-start | bytes 3276800 | tf_op jit(solution)/shard_map/all_to_all | solution.py:373
  15.9 4.2 %reshape.15 = bf16[8,342,768]{2,1,0:T(8,128)(2,1)} reshape(bf16[1,2736,768]{2,1,0:T(8,128)(2,1)} %param.6) | data formatting | bytes 8404992 | tf_op jit(solution)/shard_map/reshape | solution.py:375
  20.0 2.0 %fusion = bf16[8,352,768]{2,1,0:T(8,128)(2,1)} fusion(s32[]{:T(128)S(6)} %select_n.63, bf16[8,342,768]{2,1,0:T(8,128)(2,1)} %reshape.15), kind=kLoop, calls=%fused_computation.8 | loop fusion | bytes 4743172
  22.1 0.5 copy-done.1
  22.6 0.8 fusion.1
  23.4 0.9 fusion.2
  24.3 0.9 fusion.3
  25.2 0.9 fusion.4
  26.0 0.8 fusion.5
  26.9 0.8 fusion.6
  27.7 0.8 fusion.7
  28.5 27.9 %all-to-all-done.recv_ref.mine_rows = bf16[32,200,128]{2,1,0:T(8,128)(2,1)S(1)} async-done(((bf16[32,200,128]{2,1,0:T(8,128)(2,1)}), bf16[32,200,128]{2,1,0:T(8,128)(2,1)S(1)}, u32[]{:S(2)}, u32[]{:S(2)}) %all-to-all-start) | async-done | bytes 1638432 | tf_op jit(solution)/shard_map/all_to_all | solution.py:373
  56.4 17.4 %shard_map.77 = (bf16[32,200,128]{2,1,0:T(8,128)(2,1)}, bf16[1024,2176]{1,0:T(8,128)(2,1)}, bf16[1024,1408]{1,0:T(8,128)(2,1)}) custom-call(bf16[32,200,128]{2,1,0:T(8,128)(2,1)S(1)} %all-to-all-done.recv_ref.mine_rows, bf16[2816,768]{1,0:T(8,128)(2,1)} %bitcast.2.table_ref, f32[2,128]{1,0:T(2,128)S(1)} %copy-done), custom_call_target="tpu_custom_call" | custom-call | tf_op jit(solution)/shard_map/pallas_call | solution.py:381
  73.9 0.1 collective-permute-start
  74.0 5.7 %all-to-all-start.1 = ((bf16[32,200,128]{2,1,0:T(8,128)(2,1)}), bf16[32,200,128]{2,1,0:T(8,128)(2,1)S(1)}, u32[]{:S(2)}, u32[]{:S(2)}) async-start(bf16[32,200,128]{2,1,0:T(8,128)(2,1)} %get-tuple-element.16), calls=%async_computation.1 | async-start | bytes 3276800 | tf_op jit(solution)/shard_map/all_to_all | solution.py:407
  79.7 2.1 %collective-permute-done.other_in = bf16[1024,2176]{1,0:T(8,128)(2,1)} collective-permute-done((bf16[1024,2176]{1,0:T(8,128)(2,1)}, bf16[1024,2176]{1,0:T(8,128)(2,1)}, u32[]{:S(2)}, u32[]{:S(2)}) %collective-permute-start) | collective-permute-done | bytes 4456480 | tf_op jit(solution)/shard_map/ppermute | solution.py:410
  81.8 10.3 %shard_map.78 = (f32[352,768]{1,0:T(8,128)}, bf16[352,768]{1,0:T(8,128)(2,1)}, bf16[352,768]{1,0:T(8,128)(2,1)}, bf16[352,768]{1,0:T(8,128)(2,1)}) custom-call(bf16[1024,1408]{1,0:T(8,128)(2,1)} %get-tuple-element.18.mine_in, bf16[1024,2176]{1,0:T(8,128)(2,1)} %collective-permute-done.other_in, bf16[32,200,128]{2,1,0:T(8,128)(2,1)S(1)} %all-to-all-done.recv_ref.mine_rows), custom_call_target="tpu_custom_call" | custom-call | flops 1 | bytes 1 | tf_op jit(solution)/shard_map/pallas_call | solution.py:411
  92.2 2.2 %collective-permute-start.1 = (bf16[352,768]{1,0:T(8,128)(2,1)}, bf16[352,768]{1,0:T(8,128)(2,1)S(1)}, u32[]{:S(2)}, u32[]{:S(2)}) collective-permute-start(bf16[352,768]{1,0:T(8,128)(2,1)} %get-tuple-element.21), channel_id=1, source_target_pairs={{0,128},{32,160},{64,192},{96,224},{128,0},{160,32},{192,64},{224,... | collective-permute-start | bytes 1622024 | tf_op jit(solution)/shard_map/ppermute | solution.py:431
  94.4 2.0 %collective-permute-start.3 = (bf16[352,768]{1,0:T(8,128)(2,1)}, bf16[352,768]{1,0:T(8,128)(2,1)S(1)}, u32[]{:S(2)}, u32[]{:S(2)}) collective-permute-start(bf16[352,768]{1,0:T(8,128)(2,1)} %get-tuple-element.23), channel_id=1, source_target_pairs={{0,192},{32,224},{64,0},{96,32},{128,64},{160,96},{192,128},{224,1... | collective-permute-start | bytes 1622024 | tf_op jit(solution)/shard_map/ppermute | solution.py:431
  96.4 24.5 %all-to-all-done.1.got_ref = bf16[32,200,128]{2,1,0:T(8,128)(2,1)S(1)} async-done(((bf16[32,200,128]{2,1,0:T(8,128)(2,1)}), bf16[32,200,128]{2,1,0:T(8,128)(2,1)S(1)}, u32[]{:S(2)}, u32[]{:S(2)}) %all-to-all-start.1) | async-done | bytes 1638432 | tf_op jit(solution)/shard_map/all_to_all | solution.py:407
  120.9 0.0 collective-permute-done.1.first_ref
  120.9 0.0 collective-permute-done.2.second_ref
  120.9 2.9 %shard_map.79 = (bf16[128,768]{1,0:T(8,128)(2,1)}, f32[1,128]{1,0:T(1,128)}, bf16[342,768]{1,0:T(8,128)(2,1)}) custom-call(bf16[32,200,128]{2,1,0:T(8,128)(2,1)S(1)} %all-to-all-done.1.got_ref, bf16[1024,128]{1,0:T(8,128)(2,1)} %get-tuple-element.17.pick_in, f32[352,768]{1,0:T(8,128)} %get-tuple-element.20.share_in, ...), custom_call_target="tpu_custom_call" | custom-call | tf_op jit(solution)/shard_map/pallas_call | solution.py:433
  (5 shorter events, 0.0 us)
Async XLA Ops:
  4.3 52.2 %all-to-all-start = ((bf16[32,200,128]{2,1,0:T(8,128)(2,1)}), bf16[32,200,128]{2,1,0:T(8,128)(2,1)S(1)}, u32[]{:S(2)}, u32[]{:S(2)}) async-start(bf16[32,200,128]{2,1,0:T(8,128)(2,1)} %get-tuple-element.15), calls=%async_computation | async-start | bytes 3276800 | tf_op jit(solution)/shard_map/all_to_all | solution.py:373
  20.0 2.6 %copy-start.1 = (bf16[8,342,768]{2,1,0:T(8,128)(2,1)S(1)}, bf16[8,342,768]{2,1,0:T(8,128)(2,1)}, u32[]{:S(2)}) copy-start(bf16[8,342,768]{2,1,0:T(8,128)(2,1)} %reshape.15) | copy-start | bytes 12607492
  26.9 29.6 %copy-start = (f32[2,128]{1,0:T(2,128)S(1)}, f32[2,128]{1,0:T(2,128)}, u32[]{:S(2)}) copy-start(f32[2,128]{1,0:T(2,128)} %constant.86.clone.pads_ref) | copy-start | bytes 3076
  73.9 8.0 %collective-permute-start = (bf16[1024,2176]{1,0:T(8,128)(2,1)}, bf16[1024,2176]{1,0:T(8,128)(2,1)}, u32[]{:S(2)}, u32[]{:S(2)}) collective-permute-start(bf16[1024,2176]{1,0:T(8,128)(2,1)} %get-tuple-element.19), channel_id=1, source_target_pairs={{0,32},{32,0},{64,96},{96,64},{128,160},{160,128},{192,224},{224,1... | collective-permute-start | bytes 13369352 | tf_op jit(solution)/shard_map/ppermute | solution.py:410
  74.0 46.9 %all-to-all-start.1 = ((bf16[32,200,128]{2,1,0:T(8,128)(2,1)}), bf16[32,200,128]{2,1,0:T(8,128)(2,1)S(1)}, u32[]{:S(2)}, u32[]{:S(2)}) async-start(bf16[32,200,128]{2,1,0:T(8,128)(2,1)} %get-tuple-element.16), calls=%async_computation.1 | async-start | bytes 3276800 | tf_op jit(solution)/shard_map/all_to_all | solution.py:407
  92.2 28.7 %collective-permute-start.1 = (bf16[352,768]{1,0:T(8,128)(2,1)}, bf16[352,768]{1,0:T(8,128)(2,1)S(1)}, u32[]{:S(2)}, u32[]{:S(2)}) collective-permute-start(bf16[352,768]{1,0:T(8,128)(2,1)} %get-tuple-element.21), channel_id=1, source_target_pairs={{0,128},{32,160},{64,192},{96,224},{128,0},{160,32},{192,64},{224,... | collective-permute-start | bytes 1622024 | tf_op jit(solution)/shard_map/ppermute | solution.py:431
  94.4 26.5 %collective-permute-start.2 = (bf16[352,768]{1,0:T(8,128)(2,1)}, bf16[352,768]{1,0:T(8,128)(2,1)S(1)}, u32[]{:S(2)}, u32[]{:S(2)}) collective-permute-start(bf16[352,768]{1,0:T(8,128)(2,1)} %get-tuple-element.22), channel_id=1, source_target_pairs={{0,64},{32,96},{64,128},{96,160},{128,192},{160,224},{192,0},{224,... | collective-permute-start | bytes 1622024 | tf_op jit(solution)/shard_map/ppermute | solution.py:431
  94.4 26.5 %collective-permute-start.3 = (bf16[352,768]{1,0:T(8,128)(2,1)}, bf16[352,768]{1,0:T(8,128)(2,1)S(1)}, u32[]{:S(2)}, u32[]{:S(2)}) collective-permute-start(bf16[352,768]{1,0:T(8,128)(2,1)} %get-tuple-element.23), channel_id=1, source_target_pairs={{0,192},{32,224},{64,0},{96,32},{128,64},{160,96},{192,128},{224,1... | collective-permute-start | bytes 1622024 | tf_op jit(solution)/shard_map/ppermute | solution.py:431

commit v5 on v4

--- a/solution.py
+++ b/solution.py
@@ -37,11 +37,11 @@
 
 
 def pack_kernel(
-    labels, shards, embed_ref, short_ref, pos_ref, send_out, pick_ref, held_ref, sem
+    labels, shards, embed_ref, short_ref, pos_ref, send_ref, pick_ref
 ):
     rows, width = embed_ref.shape
     slots_k = short_ref.shape[0]
-    clusters = send_out.shape[0]
+    clusters = send_ref.shape[0]
     cap = CAP
     block = labels // shards
     place = lax.axis_index("rows")
@@ -86,30 +86,20 @@
     got_names = dot(pick, names, NT)
     own = lax.shift_right_logical(iota(got_values.shape, 0), 5).astype(F32)
     kept = jnp.where(got_names == own, got_values, 0.0)
-    kept = kept.reshape(clusters, cap // GROUP, GROUP, LANES)
     source = iota((LANES, LANES), 0)
-    folded = jnp.bitwise_and(source, 2 * count - 1)
-    folded = jnp.where(source < used, folded, LANES)
     target = iota((LANES, LANES), 1)
-    meta = jnp.zeros((clusters * GROUP, LANES), F32)
-    for g in range(cap // GROUP):
-        fold = (folded + g * GROUP_LANES == target).astype(BF)
-        part = kept[:, g].reshape(clusters * GROUP, LANES).astype(BF)
-        meta += dot(part, fold)
-    held_ref[:, width // LANES * cap :, :] = meta.astype(BF).reshape(clusters, GROUP, LANES)
-    step = clusters // 4
-    copies = []
-    for i in range(4):
-        here = slice(i * step, (i + 1) * step)
-        got = dot(pick[i * step * cap : (i + 1) * step * cap], embed_ref[...]).astype(BF)
-        for k in range(width // LANES):
-            part = got[:, k * LANES : (k + 1) * LANES]
-            held_ref[here, k * cap : (k + 1) * cap, :] = part.reshape(step, cap, LANES)
-        copy = pltpu.make_async_copy(held_ref.at[here], send_out.at[here], sem.at[i])
-        copy.start()
-        copies.append(copy)
-    for copy in copies:
-        copy.wait()
+    match = jnp.bitwise_and(source, 2 * count - 1) == jnp.bitwise_and(target, GROUP_LANES - 1)
+    fold = jnp.logical_and(source < used, match).astype(BF)
+    found = dot(kept.astype(BF), fold).reshape(clusters, cap // GROUP, GROUP, LANES)
+    group = iota((clusters, GROUP, LANES), 2) // GROUP_LANES
+    meta = found[:, 0]
+    for g in range(1, cap // GROUP):
+        meta = jnp.where(group == g, found[:, g], meta)
+    send_ref[:, width // LANES * cap :, :] = meta.astype(BF)
+    got = dot(pick, embed_ref[...]).astype(BF)
+    for k in range(width // LANES):
+        part = got[:, k * LANES : (k + 1) * LANES]
+        send_ref[:, k * cap : (k + 1) * cap, :] = part.reshape(clusters, cap, LANES)
 
 
 def assemble(recv_ref, rows_ref):
@@ -247,49 +237,36 @@
         copy.wait()
 
 
-def weight_kernel(
-    mine_in, other_in, mine_rows, share_out, first_out, second_out, third_out,
-    mine_ref, other_ref, rows_ref, share_ref, parts_ref, load_sem, store_sem,
-):
-    half = mine_ref.shape[1]
-    middle = half // 2 // LANES * LANES
-    upper, lower = slice(middle, half), slice(0, middle)
+def weight_kernel(blocks, mine_in, other_in, mine_rows, *rest):
+    outs, scratch = rest[: len(blocks)], rest[len(blocks) :]
+    mine_ref, other_ref, partner_ref, rows_ref, held_ref, load_sem, store_sem = scratch
+    half = mine_in.shape[1]
+    block, width = outs[0].shape
+    first = min(blocks) * block // LANES * LANES
+    last = -(-(max(blocks) + 1) * block // LANES) * LANES
+    here = slice(first, last)
     loads = []
-    for source, target, here in (
-        (mine_in, mine_ref, upper),
-        (other_in, other_ref, slice(half, None)),
-        (other_in, other_ref, upper),
-        (mine_in, mine_ref, lower),
-        (other_in, other_ref, lower),
+    for source, target in (
+        (mine_in.at[:, here], mine_ref),
+        (other_in.at[:, half:], partner_ref),
+        (other_in.at[:, here], other_ref),
     ):
-        load = pltpu.make_async_copy(
-            source.at[:, here], target.at[:, here], load_sem.at[len(loads)]
-        )
+        load = pltpu.make_async_copy(source, target, load_sem.at[len(loads)])
         load.start()
         loads.append(load)
     assemble(mine_rows, rows_ref)
-    block = share_ref.shape[0]
     stores = []
-    for i, (k, out) in enumerate(
-        ((2, second_out), (3, third_out), (1, first_out), (0, share_out))
-    ):
-        here = slice(k * block, (k + 1) * block)
-        if i in (0, 2):
-            loads[3 * (i // 2)].wait()
-        grads = dot(mine_ref[:, here], rows_ref[...], TN)
+    for i, k in enumerate(blocks):
+        at = slice(k * block - first, (k + 1) * block - first)
+        if i == 0:
+            loads[0].wait()
+        grads = dot(mine_ref[:, at], rows_ref[...], TN)
         if i == 0:
             loads[1].wait()
             loads[2].wait()
-        if i == 2:
-            loads[4].wait()
-        grads += dot(other_ref[:, here], other_ref[:, half:], TN)
-        if k == 0:
-            share_ref[...] = grads
-            held = share_ref
-        else:
-            held = parts_ref.at[k - 1]
-            held[...] = grads.astype(BF)
-        store = pltpu.make_async_copy(held, out, store_sem.at[i])
+        grads += dot(other_ref[:, at], partner_ref[...], TN)
+        held_ref[i] = grads.astype(held_ref.dtype)
+        store = pltpu.make_async_copy(held_ref.at[i], outs[i], store_sem.at[i])
         store.start()
         stores.append(store)
     for store in stores:
@@ -297,36 +274,38 @@
 
 
 def combine_kernel(
-    scale, got_ref, pick_in, share_in, first_ref, second_ref, third_ref,
-    grad_ref, loss_ref, weight_ref, pick_ref, share_ref, sem,
+    scale, got_ref, pick_in, share_in, first_in, second_in, third_in,
+    grad_out, loss_ref, weight_ref, pick_ref, share_ref, parts_ref, grad_ref, sem,
 ):
     clusters = got_ref.shape[0]
-    width = grad_ref.shape[1]
-    rows = grad_ref.shape[0]
+    rows, width = grad_ref.shape
     loads = [pltpu.make_async_copy(pick_in, pick_ref, sem.at[0])]
     loads.append(pltpu.make_async_copy(share_in, share_ref, sem.at[1]))
+    for k, part in enumerate((first_in, second_in, third_in)):
+        loads.append(pltpu.make_async_copy(part, parts_ref.at[k], sem.at[2 + k]))
     for load in loads:
         load.start()
-    loads[1].wait()
-    summed = share_ref[...]
-    for part in (first_ref, second_ref, third_ref):
-        summed += part[...].astype(F32)
-    weight_ref[...] = summed[: weight_ref.shape[0]].astype(BF)
-    loads[0].wait()
     parts = []
     for k in range(width // LANES):
         part = got_ref[:, k * CAP : (k + 1) * CAP, :]
         parts.append(part.reshape(clusters * CAP, LANES))
-    grads = dot(pick_ref[...], jnp.concatenate(parts, axis=1), TN)
-    grad_ref[...] = grads.astype(BF)
-    terms = got_ref[:, width // LANES * CAP :, :].reshape(clusters * GROUP, LANES)
-    pick = pick_ref[...].astype(F32).reshape(clusters, CAP // GROUP, GROUP, rows)
-    loss = jnp.zeros((1, rows), F32)
-    for g in range(CAP // GROUP):
-        chosen = pick[:, g].reshape(clusters * GROUP, rows).astype(BF)
-        found = dot(terms, chosen, TN)
-        loss += jnp.sum(found[4 * g : 4 * g + 4], axis=0, keepdims=True)
-    loss_ref[...] = loss * scale
+    terms = got_ref[:, width // LANES * CAP :, :].astype(F32)
+    group = lax.shift_right_logical(iota((clusters, GROUP, LANES), 2), 2)
+    spread = [jnp.where(group == g, terms, 0.0) for g in range(CAP // GROUP)]
+    parts.append(jnp.stack(spread, axis=1).reshape(clusters * CAP, LANES).astype(BF))
+    loads[0].wait()
+    summed = dot(pick_ref[...], jnp.concatenate(parts, axis=1), TN)
+    grad_ref[...] = summed[:, :width].astype(BF)
+    store = pltpu.make_async_copy(grad_ref, grad_out, sem.at[len(loads)])
+    store.start()
+    loss_ref[...] = jnp.sum(summed[:, width:].T, axis=0, keepdims=True) * scale
+    for load in loads[1:]:
+        load.wait()
+    share = share_ref[...]
+    for k in range(parts_ref.shape[0]):
+        share += parts_ref[k].astype(F32)
+    weight_ref[...] = share[: weight_ref.shape[0]].astype(BF)
+    store.wait()
 
 
 def whole(shape, dtype):
@@ -364,10 +343,9 @@
 
     send, pick = pl.pallas_call(
         functools.partial(pack_kernel, labels, shards),
-        out_shape=(pltpu.HBM(shape, BF), whole((total, rows), BF)),
+        out_shape=(whole(shape, BF), whole((total, rows), BF)),
         in_specs=[VM] * 3,
-        out_specs=(HBM, VM),
-        scratch_shapes=[pltpu.VMEM(shape, BF), pltpu.SemaphoreType.DMA((4,))],
+        out_specs=(VM, VM),
         compiler_params=pltpu.CompilerParams(vmem_limit_bytes=60 * 1024 * 1024),
     )(embed, shortlist.T, positives.T)
     recv = lax.all_to_all(send, "clus", 0, 0, tiled=True)
@@ -408,40 +386,51 @@
 
     swap = [(i, i ^ 1) for i in range(shards)]
     other = lax.ppermute(give, "rows", swap)
-    share, *pieces = pl.pallas_call(
-        weight_kernel,
-        out_shape=(pltpu.HBM((tall, width), F32),) + (pltpu.HBM((tall, width), BF),) * 3,
-        in_specs=[HBM, HBM, VM],
-        out_specs=(HBM,) * 4,
-        scratch_shapes=[
-            pltpu.VMEM((total, half * tall), BF),
-            pltpu.VMEM((total, half * tall + width), BF),
-            pltpu.VMEM((total, width), BF),
-            pltpu.VMEM((tall, width), F32),
-            pltpu.VMEM((half - 1, tall, width), BF),
-            pltpu.SemaphoreType.DMA((5,)),
-            pltpu.SemaphoreType.DMA((4,)),
-        ],
-        compiler_params=PARAMS,
-        cost_estimate=pl.CostEstimate(flops=1, bytes_accessed=1, transcendentals=0),
-    )(in_hbm(keep), in_hbm(other), recv)
+    def weight_part(blocks, dtype):
+        first = min(blocks) * tall // LANES * LANES
+        size = -(-(max(blocks) + 1) * tall // LANES) * LANES - first
+        return pl.pallas_call(
+            functools.partial(weight_kernel, blocks),
+            out_shape=(pltpu.HBM((tall, width), dtype),) * len(blocks),
+            in_specs=[HBM, HBM, VM],
+            out_specs=(HBM,) * len(blocks),
+            scratch_shapes=[
+                pltpu.VMEM((total, size), BF),
+                pltpu.VMEM((total, size), BF),
+                pltpu.VMEM((total, width), BF),
+                pltpu.VMEM((total, width), BF),
+                pltpu.VMEM((len(blocks), tall, width), dtype),
+                pltpu.SemaphoreType.DMA((3,)),
+                pltpu.SemaphoreType.DMA((len(blocks),)),
+            ],
+            compiler_params=pltpu.CompilerParams(vmem_limit_bytes=20 * 1024 * 1024),
+            cost_estimate=pl.CostEstimate(flops=1, bytes_accessed=1, transcendentals=0),
+        )(in_hbm(keep), in_hbm(other), recv)
+
+    away = tuple(range(1, half))
     arrived = []
-    for k in (2, 1, 3):
+    for k, piece in zip(away, weight_part(away, BF)):
         perm = [(i, (i + 2 * k) % shards) for i in range(shards)]
-        arrived.append(lax.ppermute(pieces[k - 1], "rows", perm))
-
+        arrived.append(lax.ppermute(piece, "rows", perm))
+    (share,) = weight_part((0,), F32)
     row_grad, row_loss, weight_grad = pl.pallas_call(
         functools.partial(combine_kernel, 1.0 / (slots_k * labels)),
-        out_shape=(whole((rows, width), BF), whole((1, rows), F32), whole((block, width), BF)),
-        in_specs=[VM, HBM, HBM, VM, VM, VM],
-        out_specs=(VM, VM, VM),
+        out_shape=(
+            pltpu.HBM((rows, width), BF),
+            whole((1, rows), F32),
+            whole((block, width), BF),
+        ),
+        in_specs=[VM] + [HBM] * 5,
+        out_specs=(HBM, VM, VM),
         scratch_shapes=[
             pltpu.VMEM((total, rows), BF),
             pltpu.VMEM((tall, width), F32),
-            pltpu.SemaphoreType.DMA((2,)),
+            pltpu.VMEM((half - 1, tall, width), BF),
+            pltpu.VMEM((rows, width), BF),
+            pltpu.SemaphoreType.DMA((6,)),
         ],
-        compiler_params=PARAMS,
-    )(got, in_hbm(pick), in_hbm(share), *arrived)
+        compiler_params=pltpu.CompilerParams(vmem_limit_bytes=24 * 1024 * 1024),
+    )(got, in_hbm(pick), in_hbm(share), *[in_hbm(part) for part in arrived])
     return row_grad, row_loss.reshape(rows), weight_grad[None]
 
 

time: 124 us -> 124 us (level)
  waiting for transfers between devices: 54.6 us -> 51.3 us
  Pallas kernels: 34.3 us -> 36.4 us
    all_to_all x1, waiting for transfers between devices: 24.5 us -> 21.2 us  [local(): got = lax.all_to_all(back, 'clus', 0, 0, tiled=True)]
    pallas_call x1 -> x2, Pallas kernels: 10.3 us -> 13 us  [weight_part(): pl.pallas_call(functools.partial(weight_kernel, blocks), out_shape=(pltpu...]
  transfers between devices with their start and end apart: 6 -> 6, of which waited for: 3 -> 3; matrix products, arithmetic and copies ran while one was open for 10% -> 10% of each run, Pallas kernels for 8% -> 11%
where the time goes in v5:
time: 124 us; the launch traced here: 123 us
  waiting for transfers between devices  51.3 us (41%)
  Pallas kernels  36.4 us (29%)
  starting transfers between devices  22.1 us (18%)
  local copies, waits for them, and re-layouts  12.6 us (10%)
    all_to_all x1, waiting for transfers between devices, local(): recv = lax.all_to_all(send, 'clus', 0, 0, tiled=True)  27.9 us
    all_to_all x1, waiting for transfers between devices, local(): got = lax.all_to_all(back, 'clus', 0, 0, tiled=True)  21.2 us
    pallas_call x1, Pallas kernels, local(): pl.pallas_call(functools.partial(score_kernel, count), out_shape=(pltpu.H...  17.4 us
    pallas_call x2, Pallas kernels, weight_part(): pl.pallas_call(functools.partial(weight_kernel, blocks), out_shape=(pltpu...  13 us
    all_to_all x1, starting transfers between devices, local(): recv = lax.all_to_all(send, 'clus', 0, 0, tiled=True)  11.5 us
    unnamed x11, local copies, waits for them, and re-layouts  7.64 us
    all_to_all x1, starting transfers between devices, local(): got = lax.all_to_all(back, 'clus', 0, 0, tiled=True)  5.66 us
    ppermute x3, starting transfers between devices, local(): arrived.append(lax.ppermute(piece, 'rows', perm))  4.82 us
  transfers between devices with their start and end apart: 6, of which 3 were waited for; matrix products, arithmetic and copies ran while one was open for 10% of the time, Pallas kernels for 11%

profile of v5, /device:TPU:2, one launch (start us, length us, event | category | flops | bytes accessed | tf_op | source)
XLA Modules:
  0.0 123.4 jit_solution(4579027670117707351)
XLA Ops:
  0.6 3.1 %shard_map.76 = (bf16[32,200,128]{2,1,0:T(8,128)(2,1)}, bf16[1024,128]{1,0:T(8,128)(2,1)}) custom-call(bf16[128,768]{1,0:T(8,128)(2,1)} %embed_ref.1, s32[4,128]{1,0:T(4,128)} %bitcast.6, s32[8,128]{1,0:T(8,128)} %bitcast.5), custom_call_target="tpu_custom_call" | custom-call | tf_op jit(solution)/shard_map/pallas_call | solution.py:344
  3.7 11.5 %all-to-all-start = ((bf16[32,200,128]{2,1,0:T(8,128)(2,1)}), bf16[32,200,128]{2,1,0:T(8,128)(2,1)S(1)}, u32[]{:S(2)}, u32[]{:S(2)}) async-start(bf16[32,200,128]{2,1,0:T(8,128)(2,1)} %get-tuple-element.14), calls=%async_computation | async-start | bytes 3276800 | tf_op jit(solution)/shard_map/all_to_all | solution.py:351
  15.3 4.2 %reshape.15 = bf16[8,342,768]{2,1,0:T(8,128)(2,1)} reshape(bf16[1,2736,768]{2,1,0:T(8,128)(2,1)} %param.6) | data formatting | bytes 8404992 | tf_op jit(solution)/shard_map/reshape | solution.py:353
  19.5 2.0 %fusion = bf16[8,352,768]{2,1,0:T(8,128)(2,1)} fusion(s32[]{:T(128)S(6)} %select_n.63, bf16[8,342,768]{2,1,0:T(8,128)(2,1)} %reshape.15), kind=kLoop, calls=%fused_computation.8 | loop fusion | bytes 4743172
  21.5 0.5 copy-done.1
  22.0 0.8 fusion.1
  22.9 0.9 fusion.2
  23.8 0.9 fusion.3
  24.6 0.9 fusion.4
  25.5 0.8 fusion.5
  26.3 0.8 fusion.6
  27.1 0.8 fusion.7
  28.0 27.9 %all-to-all-done.recv_ref.mine_rows = bf16[32,200,128]{2,1,0:T(8,128)(2,1)S(1)} async-done(((bf16[32,200,128]{2,1,0:T(8,128)(2,1)}), bf16[32,200,128]{2,1,0:T(8,128)(2,1)S(1)}, u32[]{:S(2)}, u32[]{:S(2)}) %all-to-all-start) | async-done | bytes 1638432 | tf_op jit(solution)/shard_map/all_to_all | solution.py:351
  55.9 17.4 %shard_map.77 = (bf16[32,200,128]{2,1,0:T(8,128)(2,1)}, bf16[1024,2176]{1,0:T(8,128)(2,1)}, bf16[1024,1408]{1,0:T(8,128)(2,1)}) custom-call(bf16[32,200,128]{2,1,0:T(8,128)(2,1)S(1)} %all-to-all-done.recv_ref.mine_rows, bf16[2816,768]{1,0:T(8,128)(2,1)} %bitcast.2.table_ref, f32[2,128]{1,0:T(2,128)S(1)} %copy-done), custom_call_target="tpu_custom_call" | custom-call | tf_op jit(solution)/shard_map/pallas_call | solution.py:359
  73.3 0.1 collective-permute-start
  73.4 5.7 %all-to-all-start.1 = ((bf16[32,200,128]{2,1,0:T(8,128)(2,1)}), bf16[32,200,128]{2,1,0:T(8,128)(2,1)S(1)}, u32[]{:S(2)}, u32[]{:S(2)}) async-start(bf16[32,200,128]{2,1,0:T(8,128)(2,1)} %get-tuple-element.15), calls=%async_computation.1 | async-start | bytes 3276800 | tf_op jit(solution)/shard_map/all_to_all | solution.py:385
  79.1 2.2 %collective-permute-done.other_in = bf16[1024,2176]{1,0:T(8,128)(2,1)} collective-permute-done((bf16[1024,2176]{1,0:T(8,128)(2,1)}, bf16[1024,2176]{1,0:T(8,128)(2,1)}, u32[]{:S(2)}, u32[]{:S(2)}) %collective-permute-start) | collective-permute-done | bytes 4456480 | tf_op jit(solution)/shard_map/ppermute | solution.py:388
  81.3 8.7 %shard_map.79 = (bf16[352,768]{1,0:T(8,128)(2,1)}, bf16[352,768]{1,0:T(8,128)(2,1)}, bf16[352,768]{1,0:T(8,128)(2,1)}) custom-call(bf16[1024,1408]{1,0:T(8,128)(2,1)} %get-tuple-element.17.mine_in, bf16[1024,2176]{1,0:T(8,128)(2,1)} %collective-permute-done.other_in, bf16[32,200,128]{2,1,0:T(8,128)(2,1)S(1)} %all-to-all-done.recv_ref.mine_rows), custom_call_target="tpu_custom_call" | custom-call | flops 1 | bytes 1 | tf_op jit(solution)/shard_map/pallas_call | solution.py:392
  90.0 1.5 %collective-permute-start.1 = (bf16[352,768]{1,0:T(8,128)(2,1)}, bf16[352,768]{1,0:T(8,128)(2,1)}, u32[]{:S(2)}, u32[]{:S(2)}) collective-permute-start(bf16[352,768]{1,0:T(8,128)(2,1)} %get-tuple-element.19), channel_id=1, source_target_pairs={{0,64},{32,96},{64,128},{96,160},{128,192},{160,224},{192,0},{224,... | collective-permute-start | bytes 1622024 | tf_op jit(solution)/shard_map/ppermute | solution.py:414
  91.6 1.1 collective-permute-start.2
  92.7 2.2 %collective-permute-start.3 = (bf16[352,768]{1,0:T(8,128)(2,1)}, bf16[352,768]{1,0:T(8,128)(2,1)}, u32[]{:S(2)}, u32[]{:S(2)}) collective-permute-start(bf16[352,768]{1,0:T(8,128)(2,1)} %get-tuple-element.21), channel_id=1, source_target_pairs={{0,192},{32,224},{64,0},{96,32},{128,64},{160,96},{192,128},{224,1... | collective-permute-start | bytes 1622024 | tf_op jit(solution)/shard_map/ppermute | solution.py:414
  94.9 4.2 %shard_map.78.share_in = f32[352,768]{1,0:T(8,128)} custom-call(bf16[1024,1408]{1,0:T(8,128)(2,1)} %get-tuple-element.17.mine_in, bf16[1024,2176]{1,0:T(8,128)(2,1)} %collective-permute-done.other_in, bf16[32,200,128]{2,1,0:T(8,128)(2,1)S(1)} %all-to-all-done.recv_ref.mine_rows), custom_call_target="tpu_custom_call" | custom-call | flops 1 | bytes 1 | tf_op jit(solution)/shard_map/pallas_call | solution.py:392
  99.1 21.2 %all-to-all-done.1.got_ref = bf16[32,200,128]{2,1,0:T(8,128)(2,1)S(1)} async-done(((bf16[32,200,128]{2,1,0:T(8,128)(2,1)}), bf16[32,200,128]{2,1,0:T(8,128)(2,1)S(1)}, u32[]{:S(2)}, u32[]{:S(2)}) %all-to-all-start.1) | async-done | bytes 1638432 | tf_op jit(solution)/shard_map/all_to_all | solution.py:385
  120.3 3.0 %shard_map.80 = (bf16[128,768]{1,0:T(8,128)(2,1)}, f32[1,128]{1,0:T(1,128)}, bf16[342,768]{1,0:T(8,128)(2,1)}) custom-call(bf16[32,200,128]{2,1,0:T(8,128)(2,1)S(1)} %all-to-all-done.1.got_ref, bf16[1024,128]{1,0:T(8,128)(2,1)} %get-tuple-element.16.pick_in, f32[352,768]{1,0:T(8,128)} %shard_map.78.share_in, ...), custom_call_target="tpu_custom_call" | custom-call | tf_op jit(solution)/shard_map/pallas_call | solution.py:416
  (6 shorter events, 0.0 us)
Async XLA Ops:
  3.7 52.2 %all-to-all-start = ((bf16[32,200,128]{2,1,0:T(8,128)(2,1)}), bf16[32,200,128]{2,1,0:T(8,128)(2,1)S(1)}, u32[]{:S(2)}, u32[]{:S(2)}) async-start(bf16[32,200,128]{2,1,0:T(8,128)(2,1)} %get-tuple-element.14), calls=%async_computation | async-start | bytes 3276800 | tf_op jit(solution)/shard_map/all_to_all | solution.py:351
  19.5 2.6 %copy-start.1 = (bf16[8,342,768]{2,1,0:T(8,128)(2,1)S(1)}, bf16[8,342,768]{2,1,0:T(8,128)(2,1)}, u32[]{:S(2)}) copy-start(bf16[8,342,768]{2,1,0:T(8,128)(2,1)} %reshape.15) | copy-start | bytes 12607492
  26.3 29.6 %copy-start = (f32[2,128]{1,0:T(2,128)S(1)}, f32[2,128]{1,0:T(2,128)}, u32[]{:S(2)}) copy-start(f32[2,128]{1,0:T(2,128)} %constant.86.clone.pads_ref) | copy-start | bytes 3076
  73.3 8.0 %collective-permute-start = (bf16[1024,2176]{1,0:T(8,128)(2,1)}, bf16[1024,2176]{1,0:T(8,128)(2,1)}, u32[]{:S(2)}, u32[]{:S(2)}) collective-permute-start(bf16[1024,2176]{1,0:T(8,128)(2,1)} %get-tuple-element.18), channel_id=1, source_target_pairs={{0,32},{32,0},{64,96},{96,64},{128,160},{160,128},{192,224},{224,1... | collective-permute-start | bytes 13369352 | tf_op jit(solution)/shard_map/ppermute | solution.py:388
  73.4 46.9 %all-to-all-start.1 = ((bf16[32,200,128]{2,1,0:T(8,128)(2,1)}), bf16[32,200,128]{2,1,0:T(8,128)(2,1)S(1)}, u32[]{:S(2)}, u32[]{:S(2)}) async-start(bf16[32,200,128]{2,1,0:T(8,128)(2,1)} %get-tuple-element.15), calls=%async_computation.1 | async-start | bytes 3276800 | tf_op jit(solution)/shard_map/all_to_all | solution.py:385
  90.0 30.3 %collective-permute-start.1 = (bf16[352,768]{1,0:T(8,128)(2,1)}, bf16[352,768]{1,0:T(8,128)(2,1)}, u32[]{:S(2)}, u32[]{:S(2)}) collective-permute-start(bf16[352,768]{1,0:T(8,128)(2,1)} %get-tuple-element.19), channel_id=1, source_target_pairs={{0,64},{32,96},{64,128},{96,160},{128,192},{160,224},{192,0},{224,... | collective-permute-start | bytes 1622024 | tf_op jit(solution)/shard_map/ppermute | solution.py:414
  91.6 28.7 %collective-permute-start.2 = (bf16[352,768]{1,0:T(8,128)(2,1)}, bf16[352,768]{1,0:T(8,128)(2,1)}, u32[]{:S(2)}, u32[]{:S(2)}) collective-permute-start(bf16[352,768]{1,0:T(8,128)(2,1)} %get-tuple-element.20), channel_id=1, source_target_pairs={{0,128},{32,160},{64,192},{96,224},{128,0},{160,32},{192,64},{224,... | collective-permute-start | bytes 1622024 | tf_op jit(solution)/shard_map/ppermute | solution.py:414
  92.7 27.6 %collective-permute-start.3 = (bf16[352,768]{1,0:T(8,128)(2,1)}, bf16[352,768]{1,0:T(8,128)(2,1)}, u32[]{:S(2)}, u32[]{:S(2)}) collective-permute-start(bf16[352,768]{1,0:T(8,128)(2,1)} %get-tuple-element.21), channel_id=1, source_target_pairs={{0,192},{32,224},{64,0},{96,32},{128,64},{160,96},{192,128},{224,1... | collective-permute-start | bytes 1622024 | tf_op jit(solution)/shard_map/ppermute | solution.py:414

commit v6 on v5

--- a/solution.py
+++ b/solution.py
@@ -15,7 +15,7 @@
 GROUP = 8
 GROUP_LANES = 32
 VMEM_LIMIT = 40 * 1024 * 1024
-TALL = 32
+TALL = 16
 BLOCK = 512
 LOG2E = 1.4426950408889634
 

time: 124 us -> 123 us (level)
  no operation moved by 1% of the time
where the time goes in v6:
time: 123 us
  waiting for transfers between devices  51.3 us (42%)
  Pallas kernels  35.9 us (29%)
  starting transfers between devices  22.1 us (18%)
  local copies, waits for them, and re-layouts  12.6 us (10%)
    all_to_all x1, waiting for transfers between devices, local(): recv = lax.all_to_all(send, 'clus', 0, 0, tiled=True)  27.9 us
    all_to_all x1, waiting for transfers between devices, local(): got = lax.all_to_all(back, 'clus', 0, 0, tiled=True)  21.2 us
    pallas_call x1, Pallas kernels, local(): pl.pallas_call(functools.partial(score_kernel, count), out_shape=(pltpu.H...  16.9 us
    pallas_call x2, Pallas kernels, weight_part(): pl.pallas_call(functools.partial(weight_kernel, blocks), out_shape=(pltpu...  13 us
    all_to_all x1, starting transfers between devices, local(): recv = lax.all_to_all(send, 'clus', 0, 0, tiled=True)  11.5 us
    unnamed x11, local copies, waits for them, and re-layouts  7.64 us
    all_to_all x1, starting transfers between devices, local(): got = lax.all_to_all(back, 'clus', 0, 0, tiled=True)  5.68 us
    ppermute x3, starting transfers between devices, local(): arrived.append(lax.ppermute(piece, 'rows', perm))  4.82 us
  transfers between devices with their start and end apart: 6, of which 3 were waited for; matrix products, arithmetic and copies ran while one was open for 10% of the time, Pallas kernels for 11%

profile of v6, /device:TPU:2, one launch (start us, length us, event | category | flops | bytes accessed | tf_op | source)
XLA Modules:
  0.0 123.0 jit_solution(6312649345306172543)
XLA Ops:
  0.6 3.1 %shard_map.76 = (bf16[32,200,128]{2,1,0:T(8,128)(2,1)}, bf16[1024,128]{1,0:T(8,128)(2,1)}) custom-call(bf16[128,768]{1,0:T(8,128)(2,1)} %embed_ref.1, s32[4,128]{1,0:T(4,128)} %bitcast.6, s32[8,128]{1,0:T(8,128)} %bitcast.5), custom_call_target="tpu_custom_call" | custom-call | tf_op jit(solution)/shard_map/pallas_call | solution.py:344
  3.7 11.5 %all-to-all-start = ((bf16[32,200,128]{2,1,0:T(8,128)(2,1)}), bf16[32,200,128]{2,1,0:T(8,128)(2,1)S(1)}, u32[]{:S(2)}, u32[]{:S(2)}) async-start(bf16[32,200,128]{2,1,0:T(8,128)(2,1)} %get-tuple-element.14), calls=%async_computation | async-start | bytes 3276800 | tf_op jit(solution)/shard_map/all_to_all | solution.py:351
  15.3 4.2 %reshape.15 = bf16[8,342,768]{2,1,0:T(8,128)(2,1)} reshape(bf16[1,2736,768]{2,1,0:T(8,128)(2,1)} %param.6) | data formatting | bytes 8404992 | tf_op jit(solution)/shard_map/reshape | solution.py:353
  19.5 2.0 %fusion = bf16[8,352,768]{2,1,0:T(8,128)(2,1)} fusion(s32[]{:T(128)S(6)} %select_n.63, bf16[8,342,768]{2,1,0:T(8,128)(2,1)} %reshape.15), kind=kLoop, calls=%fused_computation.8 | loop fusion | bytes 4743172
  21.5 0.5 copy-done.1
  22.0 0.8 fusion.1
  22.9 0.9 fusion.2
  23.8 0.9 fusion.3
  24.6 0.9 fusion.4
  25.5 0.8 fusion.5
  26.3 0.8 fusion.6
  27.1 0.8 fusion.7
  28.0 27.9 %all-to-all-done.recv_ref.mine_rows = bf16[32,200,128]{2,1,0:T(8,128)(2,1)S(1)} async-done(((bf16[32,200,128]{2,1,0:T(8,128)(2,1)}), bf16[32,200,128]{2,1,0:T(8,128)(2,1)S(1)}, u32[]{:S(2)}, u32[]{:S(2)}) %all-to-all-start) | async-done | bytes 1638432 | tf_op jit(solution)/shard_map/all_to_all | solution.py:351
  55.9 16.9 %shard_map.77 = (bf16[32,200,128]{2,1,0:T(8,128)(2,1)}, bf16[1024,2176]{1,0:T(8,128)(2,1)}, bf16[1024,1408]{1,0:T(8,128)(2,1)}) custom-call(bf16[32,200,128]{2,1,0:T(8,128)(2,1)S(1)} %all-to-all-done.recv_ref.mine_rows, bf16[2816,768]{1,0:T(8,128)(2,1)} %bitcast.2.table_ref, f32[2,128]{1,0:T(2,128)S(1)} %copy-done), custom_call_target="tpu_custom_call" | custom-call | tf_op jit(solution)/shard_map/pallas_call | solution.py:359
  72.8 0.1 collective-permute-start
  72.9 5.7 %all-to-all-start.1 = ((bf16[32,200,128]{2,1,0:T(8,128)(2,1)}), bf16[32,200,128]{2,1,0:T(8,128)(2,1)S(1)}, u32[]{:S(2)}, u32[]{:S(2)}) async-start(bf16[32,200,128]{2,1,0:T(8,128)(2,1)} %get-tuple-element.15), calls=%async_computation.1 | async-start | bytes 3276800 | tf_op jit(solution)/shard_map/all_to_all | solution.py:385
  78.6 2.2 %collective-permute-done.other_in = bf16[1024,2176]{1,0:T(8,128)(2,1)} collective-permute-done((bf16[1024,2176]{1,0:T(8,128)(2,1)}, bf16[1024,2176]{1,0:T(8,128)(2,1)}, u32[]{:S(2)}, u32[]{:S(2)}) %collective-permute-start) | collective-permute-done | bytes 4456480 | tf_op jit(solution)/shard_map/ppermute | solution.py:388
  80.8 8.7 %shard_map.79 = (bf16[352,768]{1,0:T(8,128)(2,1)}, bf16[352,768]{1,0:T(8,128)(2,1)}, bf16[352,768]{1,0:T(8,128)(2,1)}) custom-call(bf16[1024,1408]{1,0:T(8,128)(2,1)} %get-tuple-element.17.mine_in, bf16[1024,2176]{1,0:T(8,128)(2,1)} %collective-permute-done.other_in, bf16[32,200,128]{2,1,0:T(8,128)(2,1)S(1)} %all-to-all-done.recv_ref.mine_rows), custom_call_target="tpu_custom_call" | custom-call | flops 1 | bytes 1 | tf_op jit(solution)/shard_map/pallas_call | solution.py:392
  89.5 1.6 %collective-permute-start.1 = (bf16[352,768]{1,0:T(8,128)(2,1)}, bf16[352,768]{1,0:T(8,128)(2,1)}, u32[]{:S(2)}, u32[]{:S(2)}) collective-permute-start(bf16[352,768]{1,0:T(8,128)(2,1)} %get-tuple-element.19), channel_id=1, source_target_pairs={{0,64},{32,96},{64,128},{96,160},{128,192},{160,224},{192,0},{224,... | collective-permute-start | bytes 1622024 | tf_op jit(solution)/shard_map/ppermute | solution.py:414
  91.1 1.1 collective-permute-start.2
  92.2 2.2 %collective-permute-start.3 = (bf16[352,768]{1,0:T(8,128)(2,1)}, bf16[352,768]{1,0:T(8,128)(2,1)}, u32[]{:S(2)}, u32[]{:S(2)}) collective-permute-start(bf16[352,768]{1,0:T(8,128)(2,1)} %get-tuple-element.21), channel_id=1, source_target_pairs={{0,192},{32,224},{64,0},{96,32},{128,64},{160,96},{192,128},{224,1... | collective-permute-start | bytes 1622024 | tf_op jit(solution)/shard_map/ppermute | solution.py:414
  94.4 4.2 %shard_map.78.share_in = f32[352,768]{1,0:T(8,128)} custom-call(bf16[1024,1408]{1,0:T(8,128)(2,1)} %get-tuple-element.17.mine_in, bf16[1024,2176]{1,0:T(8,128)(2,1)} %collective-permute-done.other_in, bf16[32,200,128]{2,1,0:T(8,128)(2,1)S(1)} %all-to-all-done.recv_ref.mine_rows), custom_call_target="tpu_custom_call" | custom-call | flops 1 | bytes 1 | tf_op jit(solution)/shard_map/pallas_call | solution.py:392
  98.6 21.2 %all-to-all-done.1.got_ref = bf16[32,200,128]{2,1,0:T(8,128)(2,1)S(1)} async-done(((bf16[32,200,128]{2,1,0:T(8,128)(2,1)}), bf16[32,200,128]{2,1,0:T(8,128)(2,1)S(1)}, u32[]{:S(2)}, u32[]{:S(2)}) %all-to-all-start.1) | async-done | bytes 1638432 | tf_op jit(solution)/shard_map/all_to_all | solution.py:385
  119.8 3.0 %shard_map.80 = (bf16[128,768]{1,0:T(8,128)(2,1)}, f32[1,128]{1,0:T(1,128)}, bf16[342,768]{1,0:T(8,128)(2,1)}) custom-call(bf16[32,200,128]{2,1,0:T(8,128)(2,1)S(1)} %all-to-all-done.1.got_ref, bf16[1024,128]{1,0:T(8,128)(2,1)} %get-tuple-element.16.pick_in, f32[352,768]{1,0:T(8,128)} %shard_map.78.share_in, ...), custom_call_target="tpu_custom_call" | custom-call | tf_op jit(solution)/shard_map/pallas_call | solution.py:416
  (6 shorter events, 0.0 us)
Async XLA Ops:
  3.7 52.2 %all-to-all-start = ((bf16[32,200,128]{2,1,0:T(8,128)(2,1)}), bf16[32,200,128]{2,1,0:T(8,128)(2,1)S(1)}, u32[]{:S(2)}, u32[]{:S(2)}) async-start(bf16[32,200,128]{2,1,0:T(8,128)(2,1)} %get-tuple-element.14), calls=%async_computation | async-start | bytes 3276800 | tf_op jit(solution)/shard_map/all_to_all | solution.py:351
  19.5 2.6 %copy-start.1 = (bf16[8,342,768]{2,1,0:T(8,128)(2,1)S(1)}, bf16[8,342,768]{2,1,0:T(8,128)(2,1)}, u32[]{:S(2)}) copy-start(bf16[8,342,768]{2,1,0:T(8,128)(2,1)} %reshape.15) | copy-start | bytes 12607492
  26.3 29.6 %copy-start = (f32[2,128]{1,0:T(2,128)S(1)}, f32[2,128]{1,0:T(2,128)}, u32[]{:S(2)}) copy-start(f32[2,128]{1,0:T(2,128)} %constant.86.clone.pads_ref) | copy-start | bytes 3076
  72.8 8.0 %collective-permute-start = (bf16[1024,2176]{1,0:T(8,128)(2,1)}, bf16[1024,2176]{1,0:T(8,128)(2,1)}, u32[]{:S(2)}, u32[]{:S(2)}) collective-permute-start(bf16[1024,2176]{1,0:T(8,128)(2,1)} %get-tuple-element.18), channel_id=1, source_target_pairs={{0,32},{32,0},{64,96},{96,64},{128,160},{160,128},{192,224},{224,1... | collective-permute-start | bytes 13369352 | tf_op jit(solution)/shard_map/ppermute | solution.py:388
  72.9 46.9 %all-to-all-start.1 = ((bf16[32,200,128]{2,1,0:T(8,128)(2,1)}), bf16[32,200,128]{2,1,0:T(8,128)(2,1)S(1)}, u32[]{:S(2)}, u32[]{:S(2)}) async-start(bf16[32,200,128]{2,1,0:T(8,128)(2,1)} %get-tuple-element.15), calls=%async_computation.1 | async-start | bytes 3276800 | tf_op jit(solution)/shard_map/all_to_all | solution.py:385
  89.5 30.3 %collective-permute-start.1 = (bf16[352,768]{1,0:T(8,128)(2,1)}, bf16[352,768]{1,0:T(8,128)(2,1)}, u32[]{:S(2)}, u32[]{:S(2)}) collective-permute-start(bf16[352,768]{1,0:T(8,128)(2,1)} %get-tuple-element.19), channel_id=1, source_target_pairs={{0,64},{32,96},{64,128},{96,160},{128,192},{160,224},{192,0},{224,... | collective-permute-start | bytes 1622024 | tf_op jit(solution)/shard_map/ppermute | solution.py:414
  91.1 28.7 %collective-permute-start.2 = (bf16[352,768]{1,0:T(8,128)(2,1)}, bf16[352,768]{1,0:T(8,128)(2,1)}, u32[]{:S(2)}, u32[]{:S(2)}) collective-permute-start(bf16[352,768]{1,0:T(8,128)(2,1)} %get-tuple-element.20), channel_id=1, source_target_pairs={{0,128},{32,160},{64,192},{96,224},{128,0},{160,32},{192,64},{224,... | collective-permute-start | bytes 1622024 | tf_op jit(solution)/shard_map/ppermute | solution.py:414
  92.2 27.6 %collective-permute-start.3 = (bf16[352,768]{1,0:T(8,128)(2,1)}, bf16[352,768]{1,0:T(8,128)(2,1)}, u32[]{:S(2)}, u32[]{:S(2)}) collective-permute-start(bf16[352,768]{1,0:T(8,128)(2,1)} %get-tuple-element.21), channel_id=1, source_target_pairs={{0,192},{32,224},{64,0},{96,32},{128,64},{160,96},{192,128},{224,1... | collective-permute-start | bytes 1622024 | tf_op jit(solution)/shard_map/ppermute | solution.py:414

commit v7 on v6

--- a/solution.py
+++ b/solution.py
@@ -10,7 +10,7 @@
 BF = jnp.bfloat16
 F32 = jnp.float32
 LANES = 128
-CHUNK = 256
+CHUNK = 512
 CAP = 32
 GROUP = 8
 GROUP_LANES = 32
@@ -137,10 +137,11 @@
 ):
     sources = recv_ref.shape[0]
     total, width = rows_ref.shape
-    chunks = weight_ref.shape[0] // CHUNK
+    labels = weight_ref.shape[0]
+    bounds = [slice(k, min(k + CHUNK, labels)) for k in range(0, labels, CHUNK)]
+    chunks = len(bounds)
     loads = []
-    for i in range(chunks):
-        here = slice(i * CHUNK, (i + 1) * CHUNK)
+    for i, here in enumerate(bounds):
         load = pltpu.make_async_copy(table_ref.at[here], weight_ref.at[here], weight_sem.at[i])
         load.start()
         loads.append(load)
@@ -151,8 +152,8 @@
     copies = [spare]
 
     def score(i, at):
-        chunk = weight_ref[i * CHUNK : (i + 1) * CHUNK]
-        s_ref[i % 2, at] = dot(rows_ref[at], chunk, NT)
+        size = bounds[i].stop - bounds[i].start
+        s_ref[i % 2, at, :size] = dot(rows_ref[at], weight_ref[bounds[i]], NT)
 
     def pointwise(i, at):
         for start in range(at.start, at.stop, TALL):
@@ -164,9 +165,9 @@
                 summed = relu
             else:
                 relu, prod, summed = relu_ref[here], prod_ref[here], sum_ref[here]
-            for part in range(CHUNK // LANES):
-                column = i * CHUNK + part * LANES
-                s = s_ref[i % 2, here, part * LANES : (part + 1) * LANES]
+            for column in range(bounds[i].start, bounds[i].stop, LANES):
+                offset = column - bounds[i].start
+                s = s_ref[i % 2, here, offset : offset + LANES]
                 hit = lax.shift_left(bits, 31 - column // LANES) < 0
                 size = jnp.abs(s)
                 e = jnp.exp2(size * -LOG2E)
@@ -375,7 +376,7 @@
             pltpu.VMEM((total, LANES), F32),
             pltpu.VMEM((total, LANES), F32),
             pltpu.VMEM((total, LANES), F32),
-            pltpu.SemaphoreType.DMA((shards * tall // CHUNK,)),
+            pltpu.SemaphoreType.DMA((-(-shards * tall // CHUNK),)),
             pltpu.SemaphoreType.DMA((2 * total // BLOCK,)),
             pltpu.SemaphoreType.DMA((total // BLOCK,)),
             pltpu.SemaphoreType.DMA,

time: 123 us -> 123 us (level)
  no operation moved by 1% of the time
where the time goes in v7:
time: 123 us
  waiting for transfers between devices  51.3 us (42%)
  Pallas kernels  36.1 us (29%)
  starting transfers between devices  22.1 us (18%)
  local copies, waits for them, and re-layouts  12.6 us (10%)
    all_to_all x1, waiting for transfers between devices, local(): recv = lax.all_to_all(send, 'clus', 0, 0, tiled=True)  27.9 us
    all_to_all x1, waiting for transfers between devices, local(): got = lax.all_to_all(back, 'clus', 0, 0, tiled=True)  21.2 us
    pallas_call x1, Pallas kernels, local(): pl.pallas_call(functools.partial(score_kernel, count), out_shape=(pltpu.H...  17 us
    pallas_call x2, Pallas kernels, weight_part(): pl.pallas_call(functools.partial(weight_kernel, blocks), out_shape=(pltpu...  13 us
    all_to_all x1, starting transfers between devices, local(): recv = lax.all_to_all(send, 'clus', 0, 0, tiled=True)  11.5 us
    unnamed x11, local copies, waits for them, and re-layouts  7.64 us
    all_to_all x1, starting transfers between devices, local(): got = lax.all_to_all(back, 'clus', 0, 0, tiled=True)  5.68 us
    ppermute x3, starting transfers between devices, local(): arrived.append(lax.ppermute(piece, 'rows', perm))  4.84 us
  transfers between devices with their start and end apart: 6, of which 3 were waited for; matrix products, arithmetic and copies ran while one was open for 10% of the time, Pallas kernels for 11%

profile of v7, /device:TPU:2, one launch (start us, length us, event | category | flops | bytes accessed | tf_op | source)
XLA Modules:
  0.0 123.1 jit_solution(13165035715685067110)
XLA Ops:
  0.6 3.1 %shard_map.76 = (bf16[32,200,128]{2,1,0:T(8,128)(2,1)}, bf16[1024,128]{1,0:T(8,128)(2,1)}) custom-call(bf16[128,768]{1,0:T(8,128)(2,1)} %embed_ref.1, s32[4,128]{1,0:T(4,128)} %bitcast.6, s32[8,128]{1,0:T(8,128)} %bitcast.5), custom_call_target="tpu_custom_call" | custom-call | tf_op jit(solution)/shard_map/pallas_call | solution.py:345
  3.7 11.5 %all-to-all-start = ((bf16[32,200,128]{2,1,0:T(8,128)(2,1)}), bf16[32,200,128]{2,1,0:T(8,128)(2,1)S(1)}, u32[]{:S(2)}, u32[]{:S(2)}) async-start(bf16[32,200,128]{2,1,0:T(8,128)(2,1)} %get-tuple-element.14), calls=%async_computation | async-start | bytes 3276800 | tf_op jit(solution)/shard_map/all_to_all | solution.py:352
  15.3 4.2 %reshape.15 = bf16[8,342,768]{2,1,0:T(8,128)(2,1)} reshape(bf16[1,2736,768]{2,1,0:T(8,128)(2,1)} %param.6) | data formatting | bytes 8404992 | tf_op jit(solution)/shard_map/reshape | solution.py:354
  19.5 2.0 %fusion = bf16[8,352,768]{2,1,0:T(8,128)(2,1)} fusion(s32[]{:T(128)S(6)} %select_n.63, bf16[8,342,768]{2,1,0:T(8,128)(2,1)} %reshape.15), kind=kLoop, calls=%fused_computation.8 | loop fusion | bytes 4743172
  21.5 0.5 copy-done.1
  22.0 0.8 fusion.1
  22.9 0.9 fusion.2
  23.8 0.9 fusion.3
  24.6 0.9 fusion.4
  25.5 0.8 fusion.5
  26.3 0.8 fusion.6
  27.1 0.8 fusion.7
  28.0 27.9 %all-to-all-done.recv_ref.mine_rows = bf16[32,200,128]{2,1,0:T(8,128)(2,1)S(1)} async-done(((bf16[32,200,128]{2,1,0:T(8,128)(2,1)}), bf16[32,200,128]{2,1,0:T(8,128)(2,1)S(1)}, u32[]{:S(2)}, u32[]{:S(2)}) %all-to-all-start) | async-done | bytes 1638432 | tf_op jit(solution)/shard_map/all_to_all | solution.py:352
  55.9 17.0 %shard_map.77 = (bf16[32,200,128]{2,1,0:T(8,128)(2,1)}, bf16[1024,2176]{1,0:T(8,128)(2,1)}, bf16[1024,1408]{1,0:T(8,128)(2,1)}) custom-call(bf16[32,200,128]{2,1,0:T(8,128)(2,1)S(1)} %all-to-all-done.recv_ref.mine_rows, bf16[2816,768]{1,0:T(8,128)(2,1)} %bitcast.2.table_ref, f32[2,128]{1,0:T(2,128)S(1)} %copy-done), custom_call_target="tpu_custom_call" | custom-call | tf_op jit(solution)/shard_map/pallas_call | solution.py:360
  72.9 0.1 collective-permute-start
  73.0 5.7 %all-to-all-start.1 = ((bf16[32,200,128]{2,1,0:T(8,128)(2,1)}), bf16[32,200,128]{2,1,0:T(8,128)(2,1)S(1)}, u32[]{:S(2)}, u32[]{:S(2)}) async-start(bf16[32,200,128]{2,1,0:T(8,128)(2,1)} %get-tuple-element.15), calls=%async_computation.1 | async-start | bytes 3276800 | tf_op jit(solution)/shard_map/all_to_all | solution.py:386
  78.7 2.2 %collective-permute-done.other_in = bf16[1024,2176]{1,0:T(8,128)(2,1)} collective-permute-done((bf16[1024,2176]{1,0:T(8,128)(2,1)}, bf16[1024,2176]{1,0:T(8,128)(2,1)}, u32[]{:S(2)}, u32[]{:S(2)}) %collective-permute-start) | collective-permute-done | bytes 4456480 | tf_op jit(solution)/shard_map/ppermute | solution.py:389
  80.9 8.7 %shard_map.79 = (bf16[352,768]{1,0:T(8,128)(2,1)}, bf16[352,768]{1,0:T(8,128)(2,1)}, bf16[352,768]{1,0:T(8,128)(2,1)}) custom-call(bf16[1024,1408]{1,0:T(8,128)(2,1)} %get-tuple-element.17.mine_in, bf16[1024,2176]{1,0:T(8,128)(2,1)} %collective-permute-done.other_in, bf16[32,200,128]{2,1,0:T(8,128)(2,1)S(1)} %all-to-all-done.recv_ref.mine_rows), custom_call_target="tpu_custom_call" | custom-call | flops 1 | bytes 1 | tf_op jit(solution)/shard_map/pallas_call | solution.py:393
  89.6 1.6 %collective-permute-start.1 = (bf16[352,768]{1,0:T(8,128)(2,1)}, bf16[352,768]{1,0:T(8,128)(2,1)}, u32[]{:S(2)}, u32[]{:S(2)}) collective-permute-start(bf16[352,768]{1,0:T(8,128)(2,1)} %get-tuple-element.19), channel_id=1, source_target_pairs={{0,64},{32,96},{64,128},{96,160},{128,192},{160,224},{192,0},{224,... | collective-permute-start | bytes 1622024 | tf_op jit(solution)/shard_map/ppermute | solution.py:415
  91.2 1.1 collective-permute-start.2
  92.3 2.2 %collective-permute-start.3 = (bf16[352,768]{1,0:T(8,128)(2,1)}, bf16[352,768]{1,0:T(8,128)(2,1)}, u32[]{:S(2)}, u32[]{:S(2)}) collective-permute-start(bf16[352,768]{1,0:T(8,128)(2,1)} %get-tuple-element.21), channel_id=1, source_target_pairs={{0,192},{32,224},{64,0},{96,32},{128,64},{160,96},{192,128},{224,1... | collective-permute-start | bytes 1622024 | tf_op jit(solution)/shard_map/ppermute | solution.py:415
  94.5 4.2 %shard_map.78.share_in = f32[352,768]{1,0:T(8,128)} custom-call(bf16[1024,1408]{1,0:T(8,128)(2,1)} %get-tuple-element.17.mine_in, bf16[1024,2176]{1,0:T(8,128)(2,1)} %collective-permute-done.other_in, bf16[32,200,128]{2,1,0:T(8,128)(2,1)S(1)} %all-to-all-done.recv_ref.mine_rows), custom_call_target="tpu_custom_call" | custom-call | flops 1 | bytes 1 | tf_op jit(solution)/shard_map/pallas_call | solution.py:393
  98.7 21.2 %all-to-all-done.1.got_ref = bf16[32,200,128]{2,1,0:T(8,128)(2,1)S(1)} async-done(((bf16[32,200,128]{2,1,0:T(8,128)(2,1)}), bf16[32,200,128]{2,1,0:T(8,128)(2,1)S(1)}, u32[]{:S(2)}, u32[]{:S(2)}) %all-to-all-start.1) | async-done | bytes 1638432 | tf_op jit(solution)/shard_map/all_to_all | solution.py:386
  119.9 3.0 %shard_map.80 = (bf16[128,768]{1,0:T(8,128)(2,1)}, f32[1,128]{1,0:T(1,128)}, bf16[342,768]{1,0:T(8,128)(2,1)}) custom-call(bf16[32,200,128]{2,1,0:T(8,128)(2,1)S(1)} %all-to-all-done.1.got_ref, bf16[1024,128]{1,0:T(8,128)(2,1)} %get-tuple-element.16.pick_in, f32[352,768]{1,0:T(8,128)} %shard_map.78.share_in, ...), custom_call_target="tpu_custom_call" | custom-call | tf_op jit(solution)/shard_map/pallas_call | solution.py:417
  (6 shorter events, 0.0 us)
Async XLA Ops:
  3.7 52.2 %all-to-all-start = ((bf16[32,200,128]{2,1,0:T(8,128)(2,1)}), bf16[32,200,128]{2,1,0:T(8,128)(2,1)S(1)}, u32[]{:S(2)}, u32[]{:S(2)}) async-start(bf16[32,200,128]{2,1,0:T(8,128)(2,1)} %get-tuple-element.14), calls=%async_computation | async-start | bytes 3276800 | tf_op jit(solution)/shard_map/all_to_all | solution.py:352
  19.5 2.6 %copy-start.1 = (bf16[8,342,768]{2,1,0:T(8,128)(2,1)S(1)}, bf16[8,342,768]{2,1,0:T(8,128)(2,1)}, u32[]{:S(2)}) copy-start(bf16[8,342,768]{2,1,0:T(8,128)(2,1)} %reshape.15) | copy-start | bytes 12607492
  26.3 29.6 %copy-start = (f32[2,128]{1,0:T(2,128)S(1)}, f32[2,128]{1,0:T(2,128)}, u32[]{:S(2)}) copy-start(f32[2,128]{1,0:T(2,128)} %constant.86.clone.pads_ref) | copy-start | bytes 3076
  72.9 8.0 %collective-permute-start = (bf16[1024,2176]{1,0:T(8,128)(2,1)}, bf16[1024,2176]{1,0:T(8,128)(2,1)}, u32[]{:S(2)}, u32[]{:S(2)}) collective-permute-start(bf16[1024,2176]{1,0:T(8,128)(2,1)} %get-tuple-element.18), channel_id=1, source_target_pairs={{0,32},{32,0},{64,96},{96,64},{128,160},{160,128},{192,224},{224,1... | collective-permute-start | bytes 13369352 | tf_op jit(solution)/shard_map/ppermute | solution.py:389
  73.0 46.9 %all-to-all-start.1 = ((bf16[32,200,128]{2,1,0:T(8,128)(2,1)}), bf16[32,200,128]{2,1,0:T(8,128)(2,1)S(1)}, u32[]{:S(2)}, u32[]{:S(2)}) async-start(bf16[32,200,128]{2,1,0:T(8,128)(2,1)} %get-tuple-element.15), calls=%async_computation.1 | async-start | bytes 3276800 | tf_op jit(solution)/shard_map/all_to_all | solution.py:386
  89.6 30.3 %collective-permute-start.1 = (bf16[352,768]{1,0:T(8,128)(2,1)}, bf16[352,768]{1,0:T(8,128)(2,1)}, u32[]{:S(2)}, u32[]{:S(2)}) collective-permute-start(bf16[352,768]{1,0:T(8,128)(2,1)} %get-tuple-element.19), channel_id=1, source_target_pairs={{0,64},{32,96},{64,128},{96,160},{128,192},{160,224},{192,0},{224,... | collective-permute-start | bytes 1622024 | tf_op jit(solution)/shard_map/ppermute | solution.py:415
  91.2 28.7 %collective-permute-start.2 = (bf16[352,768]{1,0:T(8,128)(2,1)}, bf16[352,768]{1,0:T(8,128)(2,1)}, u32[]{:S(2)}, u32[]{:S(2)}) collective-permute-start(bf16[352,768]{1,0:T(8,128)(2,1)} %get-tuple-element.20), channel_id=1, source_target_pairs={{0,128},{32,160},{64,192},{96,224},{128,0},{160,32},{192,64},{224,... | collective-permute-start | bytes 1622024 | tf_op jit(solution)/shard_map/ppermute | solution.py:415
  92.3 27.6 %collective-permute-start.3 = (bf16[352,768]{1,0:T(8,128)(2,1)}, bf16[352,768]{1,0:T(8,128)(2,1)}, u32[]{:S(2)}, u32[]{:S(2)}) collective-permute-start(bf16[352,768]{1,0:T(8,128)(2,1)} %get-tuple-element.21), channel_id=1, source_target_pairs={{0,192},{32,224},{64,0},{96,32},{128,64},{160,96},{192,128},{224,1... | collective-permute-start | bytes 1622024 | tf_op jit(solution)/shard_map/ppermute | solution.py:415
